TPU v7x, 512 devices: a whole 4x8x8 slice. The times are simulated.
512 devices in a mesh: dp: 32 (over y, z_hi), spatial: 16 (over z_lo, x, core).
Axes of the slice: x: 4, y: 8, z: 8 (z_hi: 4, z_lo: 2; z = z_hi * 2 + z_lo), core: 2. Of those that a mesh axis runs over, the one named last changes fastest.
Arguments:
- features: bfloat16 [32, 128, 128, 256], P('dp', 'spatial')
- coarse: bfloat16 [32, 32, 32, 512], P('dp', 'spatial'), may hold values from -6 to 6
- timestep: int32 [32], P('dp'), may hold values from 0 to 999
- text_ids: int32 [32, 128], replicated, may hold values from 0 to 32255
- text_table: bfloat16 [32256, 1024], P(('dp', 'spatial')), may hold values from -6 to 6
- w_mod: bfloat16 [1024, 512], replicated, may hold values from -0.1875 to 0.1875
- w_skip: bfloat16 [512, 256], replicated, may hold values from -0.25 to 0.25
- w_conv: bfloat16 [256, 2304], replicated, may hold values from -0.125 to 0.125
- cotangent: bfloat16 [32, 128, 128, 256], P('dp', 'spatial')
Outputs:
- output: bfloat16 [32, 128, 128, 256], P('dp', 'spatial')
- grad_features: bfloat16 [32, 128, 128, 256], P('dp', 'spatial')
- grad_conv: bfloat16 [256, 2304], P('dp')
- grad_mod: bfloat16 [1024, 512], P('dp')
All inputs are finite; a program needn't handle non-finite values.
Results may differ from a plain program's by a relative error of at most 0.011.
Values may be sent and summed in bfloat16 or wider, within the bound.
A program may use at most 64 MiB of HBM per device.

v0:
```python
import math

import jax
import jax.numpy as jnp
from jax import lax
from jax.sharding import PartitionSpec as P

GROUPS = 32


EPS = 1e-05
OFFSETS = ((-1, -1), (-1, 0), (-1, 1), (0, -1), (0, 0), (0, 1), (1, -1), (1, 0), (1, 1))


def padded_2(block, sides, width):
    for axis, dim in sides:
        count = lax.axis_size(axis)
        forward = [(i, i + 1) for i in range(count - 1)]
        backward = [(target, source) for source, target in forward]
        low = lax.ppermute(
            lax.slice_in_dim(block, block.shape[dim] - width, None, axis=dim), axis, forward
        )
        high = lax.ppermute(lax.slice_in_dim(block, 0, width, axis=dim), axis, backward)
        block = jnp.concatenate([low, block, high], axis=dim)
    return block


def group_average(channel_sums, total_count, groups):
    group_width = channel_sums.shape[-1] // groups
    grouped = channel_sums.reshape(channel_sums.shape[:-1] + (groups, group_width)).sum(-1) / (
        total_count * group_width
    )
    return jnp.repeat(grouped, group_width, axis=-1)


def group_moments(first_sums, square_sums, total_count, groups):
    center = group_average(first_sums, total_count, groups)
    spread = group_average(square_sums, total_count, groups) - center * center
    return (center, lax.rsqrt(spread + EPS))


def time_embed(steps, embed_width):
    half_width = embed_width // 2
    freqs = jnp.exp(-math.log(10000.0) * jnp.arange(half_width, dtype=jnp.float32) / half_width)
    angles = steps.astype(jnp.float32)[:, None] * freqs[None, :]
    return jnp.concatenate([jnp.sin(angles), jnp.cos(angles)], axis=1)


def shifted(padded, row_step, col_step, tile_rows, tile_cols):
    return padded[
        :, 1 + row_step : 1 + row_step + tile_rows, 1 + col_step : 1 + col_step + tile_cols, :
    ]


def body(features, coarse, timestep, text_ids, text_table, w_mod, w_skip, w_conv, cotangent):
    batch_dev, tile_rows, tile_cols, channels = features.shape
    coarse_width = coarse.shape[-1]
    spatial_count = lax.axis_size("spatial")
    vocab_dev = text_table.shape[0]
    first_id = lax.axis_index(("dp", "spatial")) * vocab_dev
    local_ids = text_ids - first_id
    matches = local_ids[:, :, None] == jnp.arange(vocab_dev, dtype=jnp.int32)[None, None, :]
    counts = jnp.sum(matches.astype(jnp.float32), axis=1).astype(jnp.bfloat16)
    partial_text = jnp.dot(counts, text_table, preferred_element_type=jnp.float32)
    pooled_all = lax.psum(partial_text, ("dp", "spatial"))
    own_start = lax.axis_index("dp") * batch_dev
    pooled = lax.dynamic_slice_in_dim(pooled_all, own_start, batch_dev, 0) / text_ids.shape[1]
    embed = time_embed(timestep, w_mod.shape[0]) + pooled
    silu_embed = jax.nn.silu(embed).astype(jnp.bfloat16)
    modulation = jnp.dot(silu_embed, w_mod, preferred_element_type=jnp.float32)
    gain = 1.0 + modulation[:, :channels]
    offset_term = modulation[:, channels:]
    coarse_f = coarse.astype(jnp.float32)
    coarse_sums = lax.psum(
        (jnp.sum(coarse_f, axis=(1, 2)), jnp.sum(coarse_f * coarse_f, axis=(1, 2))), "spatial"
    )
    c_center, c_scale = group_moments(
        coarse_sums[0], coarse_sums[1], coarse.shape[1] * coarse.shape[2] * spatial_count, GROUPS
    )
    coarse_act = jax.nn.silu(
        (coarse_f - c_center[:, None, None, :]) * c_scale[:, None, None, :]
    ).astype(jnp.bfloat16)
    skip_flat = jnp.dot(
        coarse_act.reshape(-1, coarse_width), w_skip, preferred_element_type=jnp.float32
    ).astype(jnp.bfloat16)
    skip_map = skip_flat.reshape(batch_dev, coarse.shape[1], coarse.shape[2], channels)
    upsampled = jnp.repeat(jnp.repeat(skip_map, 4, axis=1), 4, axis=2)
    merged = (features.astype(jnp.float32) + upsampled.astype(jnp.float32)).astype(jnp.bfloat16)
    merged_f = merged.astype(jnp.float32)
    fine_count = tile_rows * tile_cols * spatial_count
    fine_sums = lax.psum(
        (jnp.sum(merged_f, axis=(1, 2)), jnp.sum(merged_f * merged_f, axis=(1, 2))), "spatial"
    )
    f_center, f_scale = group_moments(fine_sums[0], fine_sums[1], fine_count, GROUPS)
    normed = (merged_f - f_center[:, None, None, :]) * f_scale[:, None, None, :]
    pre_act = normed * gain[:, None, None, :] + offset_term[:, None, None, :]
    hidden = jax.nn.silu(pre_act).astype(jnp.bfloat16)
    rimmed = padded_2(hidden, (("spatial", 1),), 1)
    padded = jnp.pad(rimmed, ((0, 0), (0, 0), (1, 1), (0, 0)))
    hidden_taps = [
        shifted(padded, row_step, col_step, tile_rows, tile_cols).reshape(-1, channels)
        for row_step, col_step in OFFSETS
    ]
    conv_out = jnp.zeros((batch_dev * tile_rows * tile_cols, channels), jnp.float32)
    for tap_index in range(9):
        conv_out = conv_out + jnp.dot(
            hidden_taps[tap_index],
            w_conv[:, tap_index * channels : (tap_index + 1) * channels],
            preferred_element_type=jnp.float32,
        )
    output = (merged_f + conv_out.reshape(features.shape)).astype(jnp.bfloat16)
    cot_rimmed = padded_2(cotangent, (("spatial", 1),), 1)
    cot_padded = jnp.pad(cot_rimmed, ((0, 0), (0, 0), (1, 1), (0, 0)))
    grad_hidden = jnp.zeros((batch_dev * tile_rows * tile_cols, channels), jnp.float32)
    for tap_index in range(9):
        row_step, col_step = OFFSETS[tap_index]
        piece = shifted(cot_padded, -row_step, -col_step, tile_rows, tile_cols).reshape(
            -1, channels
        )
        kernel = w_conv[:, tap_index * channels : (tap_index + 1) * channels]
        grad_hidden = grad_hidden + lax.dot_general(
            piece, kernel, (((1,), (1,)), ((), ())), preferred_element_type=jnp.float32
        )
    sigma = jax.nn.sigmoid(pre_act)
    grad_pre = grad_hidden.reshape(features.shape) * sigma * (1.0 + pre_act * (1.0 - sigma))
    grad_gain, grad_offset = lax.psum(
        (jnp.sum(grad_pre * normed, axis=(1, 2)), jnp.sum(grad_pre, axis=(1, 2))), "spatial"
    )
    mean_one = group_average(gain * grad_offset, fine_count, GROUPS)
    mean_two = group_average(gain * grad_gain, fine_count, GROUPS)
    grad_normed = grad_pre * gain[:, None, None, :]
    grad_merged = f_scale[:, None, None, :] * (
        grad_normed - mean_one[:, None, None, :] - normed * mean_two[:, None, None, :]
    )
    grad_features = (cotangent.astype(jnp.float32) + grad_merged).astype(jnp.bfloat16)
    cot_flat = cotangent.reshape(-1, channels)
    partial_weight = jnp.concatenate(
        [
            lax.dot_general(
                tap, cot_flat, (((0,), (0,)), ((), ())), preferred_element_type=jnp.float32
            )
            for tap in hidden_taps
        ],
        axis=1,
    )
    group_total = lax.psum(partial_weight, "spatial")
    weight_share = lax.psum_scatter(group_total, "dp", scatter_dimension=0, tiled=True)
    grad_conv = weight_share.astype(jnp.bfloat16)
    mod_grad = jnp.concatenate([grad_gain, grad_offset], axis=1)
    gathered_embed, gathered_grad = (
        lax.all_gather(silu_embed.astype(jnp.float32), "dp", axis=0, tiled=True),
        lax.all_gather(mod_grad, "dp", axis=0, tiled=True),
    )
    share_rows = w_mod.shape[0] // lax.axis_size("dp")
    embed_rows = lax.dynamic_slice_in_dim(
        gathered_embed, lax.axis_index("dp") * share_rows, share_rows, 1
    )
    grad_mod = jnp.dot(embed_rows.T, gathered_grad, precision=lax.Precision.HIGHEST).astype(
        jnp.bfloat16
    )
    return (output, grad_features, grad_conv, grad_mod)


def solution(mesh):
    in_specs = (
        P("dp", "spatial", None, None),
        P("dp", "spatial", None, None),
        P("dp"),
        P(),
        P(("dp", "spatial"), None),
        P(),
        P(),
        P(),
        P("dp", "spatial", None, None),
    )
    out_specs = (
        P("dp", "spatial", None, None),
        P("dp", "spatial", None, None),
        P("dp", None),
        P("dp", None),
    )
    return jax.shard_map(body, mesh=mesh, in_specs=in_specs, out_specs=out_specs, check_vma=False)
```

profile of v0, /device:TPU:32, one launch (start us, length us, event | category | flops | bytes accessed | tf_op | source)
XLA Modules:
  0.0 689.5 jit_solution(8754793665456221566)
XLA Ops:
  8.4 1.8 fusion.103
  11.1 1.3 collective-permute-start.3
  12.4 3.0 collective-permute-start.2
  16.5 56.3 %all-reduce.4 = (f32[32,16]{1,0:T(8,128)S(1)}, f32[32,16]{1,0:T(8,128)S(1)}) all-reduce(f32[32,16]{1,0:T(8,128)S(1)} %reshape.315, f32[32,16]{1,0:T(8,128)S(1)} %reshape.314), channel_id=1, replica_groups=mesh['dp'=32,'spatial'=16] {'spatial'}, use_global_device_ids=true, to_apply=%region_4.5 | all-reduce | flops 1024 | bytes 8192 | tf_op jit(solution)/shard_map/psum | solution.py:74
  74.3 1.1 convolution_convert_fusion.1
  76.0 1.3 convert_reduce_fusion
  77.5 52.9 %all-reduce.3 = (f32[32,8]{1,0:T(8,128)S(1)}, f32[32,8]{1,0:T(8,128)S(1)}) all-reduce(f32[32,8]{1,0:T(8,128)S(1)} %reshape.318, f32[32,8]{1,0:T(8,128)S(1)} %reshape.317), channel_id=1, replica_groups=mesh['dp'=32,'spatial'=16] {'spatial'}, use_global_device_ids=true, to_apply=%region_10.11 | all-reduce | flops 512 | bytes 4096 | tf_op jit(solution)/shard_map/psum | solution.py:91
  131.8 145.8 %all-reduce.7.cloned.1.call-done = f32[32,1024]{1,0:T(8,128)} async-done(((f32[32,1024]{1,0:T(8,128)}), f32[32,1024]{1,0:T(8,128)}) %all-reduce.7.cloned.1.call-update) | async-done | bytes 131088 | tf_op jit(solution)/shard_map/psum | solution.py:65
  283.2 1.7 fusion.97
  284.9 1.3 collective-permute-start.1
  286.2 3.0 collective-permute-start
  291.5 1.1 fusion.10
  292.5 1.1 fusion.9
  295.7 1.1 fusion.6
  298.9 1.1 fusion.3
  300.0 3.1 copy.62
  303.1 77.7 %all-gather = f32[32,1,1024]{2,1,0:T(1,128)S(1)} all-gather(f32[1,1,1024]{2,1,0:T(1,128)S(1)} %get-tuple-element.35), channel_id=1, replica_groups=mesh['dp'=32,'spatial'=16] {'dp'}, dimensions={0}, use_global_device_ids=true | all-gather | bytes 135168 | tf_op jit(solution)/shard_map/all_gather | solution.py:151
  385.4 1.3 fusion.2
  386.6 145.3 %reduce-scatter.4.cloned.1.call-done = f32[8,2304]{1,0:T(8,128)} async-done(((f32[256,2304]{1,0:T(8,128)}), f32[8,2304]{1,0:T(8,128)}) %reduce-scatter.4.cloned.1.call-update) | async-done | bytes 73744
  531.9 1.2 copy.63
  533.2 64.8 %all-reduce.2 = (f32[1,256]{1,0:T(1,128)S(1)}, f32[1,256]{1,0:T(1,128)S(1)}, bf16[8,2304]{0,1:T(8,128)(2,1)}) all-reduce(f32[1,256]{1,0:T(1,128)S(1)} %bitcast.175, f32[1,256]{1,0:T(1,128)S(1)} %bitcast.176, f32[8,2304]{0,1:T(8,128)S(1)} %copy.63), channel_id=1, replica_groups=mesh['dp'=32,'spatial'=16] {'spatial'}, use_global_device_ids=true, to_apply=%region_15.16 | all-reduce | flops 18944 | bytes 114688 | tf_op jit(solution)/shard_map/psum | solution.py:126
  598.8 1.9 copy.52
  600.7 78.1 %all-gather.1 = f32[32,1,512]{2,1,0:T(1,128)S(1)} all-gather(f32[1,1,512]{2,1,0:T(1,128)S(1)} %maximum_bitcast_fusion), channel_id=1, replica_groups=mesh['dp'=32,'spatial'=16] {'dp'}, dimensions={0}, use_global_device_ids=true | all-gather | bytes 67584 | tf_op jit(solution)/shard_map/all_gather | solution.py:152
  679.7 2.9 fusion.30
  (101 shorter events, 24.1 us)
Async XLA Ops:
  7.2 271.2 %copy-start = (bf16[1024,512]{1,0:T(8,128)(2,1)S(1)}, bf16[1024,512]{1,0:T(8,128)(2,1)}, u32[]{:S(2)}) copy-start(bf16[1024,512]{1,0:T(8,128)(2,1)} %param.14) | copy-start | bytes 3145732
  7.2 270.4 %all-reduce.7.cloned.1.call-start = ((), (), s32[]{:S(2)}) async-start(), calls=%async_computation.1 | async-start | bytes 262144 | tf_op jit(solution)/shard_map/psum | solution.py:65
  10.2 521.8 %reduce-scatter.4.cloned.1.call-start = ((), (), s32[]{:S(2)}) async-start(), calls=%async_computation.2 | async-start | bytes 2433024
  11.1 267.5 %collective-permute-start.3 = (bf16[1,1,128,256]{3,2,1,0:T(8,128)(2,1)S(1)}, bf16[1,1,128,256]{3,2,1,0:T(8,128)(2,1)S(1)}, u32[]{:S(2)}, u32[]{:S(2)}) collective-permute-start(bf16[1,1,128,256]{3,2,1,0:T(8,128)(2,1)S(1)} %get-tuple-element.57), channel_id=1, source_target_pairs={{1,0},{2,1},{3,2},{4,3},{5,4},{6,5},{7,6},{8,7},{9,8},{10,9},{11,1... | collective-permute-start | bytes 196616 | tf_op jit(solution)/shard_map/ppermute | solution.py:23
  12.4 266.2 %collective-permute-start.2 = (bf16[1,1,128,256]{3,2,1,0:T(8,128)(2,1)S(1)}, bf16[1,1,128,256]{3,2,1,0:T(8,128)(2,1)S(1)}, u32[]{:S(2)}, u32[]{:S(2)}) collective-permute-start(bf16[1,1,128,256]{3,2,1,0:T(8,128)(2,1)S(1)} %get-tuple-element.56), channel_id=1, source_target_pairs={{0,1},{1,2},{2,3},{3,4},{4,5},{5,6},{6,7},{7,8},{8,9},{9,10},{10,1... | collective-permute-start | bytes 196616 | tf_op jit(solution)/shard_map/ppermute | solution.py:20
  76.0 202.7 %copy-start.1 = (bf16[1,8,128,256]{3,2,1,0:T(8,128)(2,1)S(1)}, bf16[1,8,128,256]{3,2,1,0:T(8,128)(2,1)}, u32[]{:S(2)}) copy-start(bf16[1,8,128,256]{3,2,1,0:T(8,128)(2,1)} %param.17) | copy-start | bytes 1572868
  77.3 205.9 %copy-start.2 = (bf16[1,8,128,256]{3,2,1,0:T(8,128)(2,1)}, bf16[1,8,128,256]{3,2,1,0:T(8,128)(2,1)S(1)}, u32[]{:S(2)}) copy-start(bf16[1,8,128,256]{3,2,1,0:T(8,128)(2,1)S(1)} %get-tuple-element.38) | copy-start | bytes 1572868
  278.8 1.3 copy-start.6
  284.9 4.3 collective-permute-start.1
  286.2 3.9 collective-permute-start
  291.5 6.4 copy-start.4
  380.9 1.3 copy-start.7
  384.3 1.0 copy-start.5
  533.2 146.5 %copy-start.3 = (bf16[1,8,128,256]{3,2,1,0:T(8,128)(2,1)S(1)}, bf16[1,8,128,256]{3,2,1,0:T(8,128)(2,1)}, u32[]{:S(2)}) copy-start(bf16[1,8,128,256]{3,2,1,0:T(8,128)(2,1)} %copy-done.2) | copy-start | bytes 1572868
Sparse Core Ops, SparseCore 0:
  13.6 263.9 all-reduce.6
  303.2 228.6 reduce-scatter.3
where the time goes:
time: 691 us; the launch traced here: 689 us
  blocking collectives  330 us (48%)
  waiting for transfers between devices  292 us (42%)
  matrix products  20.2 us (3%)
  between operations  15.1 us (2%)
  local copies, waits for them, and re-layouts  12.5 us (2%)
  other arithmetic  11 us (2%)
  starting transfers between devices  8.73 us (1%)
    psum x1, waiting for transfers between devices, body(): pooled_all = lax.psum(partial_text, ('dp', 'spatial'))  146 us
    unnamed x3, waiting for transfers between devices  145 us
    all_gather x1, blocking collectives, body(): lax.all_gather(mod_grad, 'dp', axis=0, tiled=True)  78.1 us
    all_gather x1, blocking collectives, body(): lax.all_gather(silu_embed.astype(jnp.float32), 'dp', axis=0, tiled=True)  77.7 us
    psum x1, blocking collectives, body(): lax.psum((jnp.sum(grad_pre * normed, axis=(1, 2)), jnp.sum(grad_pre, axis...  64.8 us
    psum x1, blocking collectives, body(): lax.psum((jnp.sum(coarse_f, axis=(1, 2)), jnp.sum(coarse_f * coarse_f, ax...  56.3 us
    psum x1, blocking collectives, body(): lax.psum((jnp.sum(merged_f, axis=(1, 2)), jnp.sum(merged_f * merged_f, ax...  52.9 us
  transfers between devices with their start and end apart: 6, of which 3 were waited for; matrix products, arithmetic and copies ran while one was open for 2% of the time, Pallas kernels for 0%

commit v1 on v0

v1 whole, which is shorter than its diff:
```python
import functools
import math

import jax
import jax.numpy as jnp
from jax import lax
from jax.experimental import pallas as pl
from jax.experimental.pallas import tpu as pltpu
from jax.sharding import PartitionSpec as P

GROUPS = 32
EPS = 1e-05
MESH = pl.DeviceIdType.MESH
F32 = jnp.float32
BF16 = jnp.bfloat16
LANES = 128
VMEM_LIMIT = 62 * 1024 * 1024


def dot(a, b, dims=((1,), (0,))):
    return lax.dot_general(a, b, (dims, ((), ())), preferred_element_type=F32)


def iota(shape, axis):
    return lax.broadcasted_iota(jnp.int32, shape, axis)


def sigmoid(x):
    return 0.5 * jnp.tanh(0.5 * x) + 0.5


def group_total(tile, width):
    lane = iota(tile.shape, 1)
    step = 1
    while step < width:
        partner = jnp.where(
            (lane & step) != 0, pltpu.roll(tile, step, 1), pltpu.roll(tile, LANES - step, 1)
        )
        tile = tile + partner
        step *= 2
    return tile


def as_row(tile, first, count):
    return jnp.concatenate([tile[first + i : first + i + 1, :] for i in range(count)], axis=1)


def as_rows(row):
    return [row[:, i * LANES : (i + 1) * LANES] for i in range(row.shape[1] // LANES)]


def column_shifts(rows, spread_ref, first_row, reverse):
    width, channels = rows.shape
    column = iota(rows.shape, 0)
    earlier = jnp.where(column == 0, 0.0, pltpu.roll(rows, 1, 0)).astype(BF16)
    later = jnp.where(column == width - 1, 0.0, pltpu.roll(rows, width - 1, 0)).astype(BF16)
    left, right = (later, earlier) if reverse else (earlier, later)
    spread_ref[pl.ds(first_row, width), 0:channels] = left
    spread_ref[pl.ds(first_row, width), channels : 2 * channels] = rows.astype(BF16)
    spread_ref[pl.ds(first_row, width), 2 * channels : 3 * channels] = right


def turned_shifts(rows, turned_ref, first_pixel):
    width, channels = rows.shape
    turned = rows.T
    column = iota(turned.shape, 1)
    later = jnp.where(column == width - 1, 0.0, pltpu.roll(turned, width - 1, 1))
    earlier = jnp.where(column == 0, 0.0, pltpu.roll(turned, 1, 1))
    for i, shifted in enumerate((later, turned, earlier)):
        turned_ref[i * channels : (i + 1) * channels, pl.ds(first_pixel, width)] = shifted.astype(BF16)


def kernel(n_dp, n_sp, tile_rows, width, *refs):
    (
        time_ref, ids_hbm, feat_hbm, coarse_hbm, table_hbm, w_mod_hbm, w_skip_hbm, w_conv_hbm, cot_hbm,
        out_hbm, grad_feat_hbm, grad_conv_hbm, grad_mod_hbm,
        out_ref, grad_feat_ref, grad_conv_ref, grad_mod_ref, ids_ref,
        feat, coarse, table, w_mod, w_skip, w_conv, w_stack, cot,
        cot_edge, far_edge, hid_edge, cot_chip, cot_spread, cot_turned, hid_spread, chosen, up, merged,
        hidden, hidden_pair, grad_hid,
        fine_box, back_box, text_out, text_box, text_sum, text_dp_box, pooled, mod_out, mod_box, mod_rows,
        weight_own, cube_out, cube_box, weight_sum, tail_sum,
        tile_box, tail_box, final_box, final_tail_box,
        load_sem, store_sem, edge_send, edge_recv, send_sem, recv_sem,
    ) = refs
    channels = feat.shape[1]
    pixels = tile_rows * width
    half = channels // 2
    part = channels // n_dp
    dp = lax.axis_index("dp")
    sp = lax.axis_index("spatial")
    chip, core = sp // 2, sp % 2
    other_sp = sp + 1 - 2 * core

    y, z_high = dp // 4, dp % 4
    z_low, x = sp // 8, chip % 4
    z = 2 * z_high + z_low
    odd_x, odd_y, odd_z = x % 2, y % 2, z_low
    high_x, high_y = x // 2, y // 2
    quarter = 2 * odd_z + odd_x
    rank = high_x * 16 + high_y * 4 + z_high

    def block_of(high):
        return 2 * (high % 2) + high // 2

    def neighbour(side, d):
        dx, dy, dz = d % 2, (d // 2) % 2, d // 4
        x_there = (x + dx * (1 - 2 * odd_x) * (1 - 2 * side) + 4) % 4
        y_there = (y + dy * (1 - 2 * odd_y) * (1 - 2 * side) + 8) % 8
        z_there = (z + dz * (1 - 2 * odd_z) * (1 - 2 * side) + 8) % 8
        return (y_there * 4 + z_there // 2, (z_there % 2) * 8 + x_there * 2 + core)

    def of_rank(number):
        x_there, y_there, z_there = number // 16, (number // 4) % 4, number % 4
        return ((2 * y_there + odd_y) * 4 + z_there, z_low * 8 + (2 * x_there + odd_x) * 2 + core)

    owns_tail = jnp.logical_and(high_y == quarter, high_x == 0)
    owner = dp // 2 == sp
    (
        FINE, BACK, TEXT, TEXT_DP, POOLED, MOD, GRAD_MOD, TILE, TAIL, FINAL, FINAL_TAIL,
        PAIR_COT, PAIR_HIDDEN, FAR, CUBE,
    ) = range(15)

    def load(source, target, index):
        return pltpu.make_async_copy(source, target, load_sem.at[index])

    own_lanes = pl.ds(pl.multiple_of(core * half, half), half)
    other_lanes = pl.ds(pl.multiple_of((1 - core) * half, half), half)
    own_pixels = pl.multiple_of(core * pixels, pixels)
    other_pixels = pl.multiple_of((1 - core) * pixels, pixels)
    own_rows = pl.ds(pl.multiple_of(width + core * pixels, width), pixels)
    loads = [
        load(ids_hbm, ids_ref, 1),
        load(table_hbm, table, 2),
        load(coarse_hbm, coarse, 0),
        load(cot_hbm, cot, 3),
        load(cot_hbm.at[:, own_lanes], cot_chip.at[own_rows], 4),
    ]
    later = [
        load(feat_hbm, feat, 5),
        load(w_skip_hbm, w_skip, 6),
        load(w_mod_hbm, w_mod, 7),
        load(w_conv_hbm, w_conv, 8),
    ]
    stacks = [
        load(
            w_conv_hbm.at[:, pl.ds(tap * channels, channels)],
            w_stack.at[pl.ds(tap * channels, channels), :],
            9 + tap,
        )
        for tap in range(9)
    ]
    for copy in loads:
        copy.start()

    barrier = pltpu.get_barrier_semaphore()

    def greet(place):
        pl.semaphore_signal(barrier, inc=1, device_id=place, device_id_type=MESH)

    @pl.loop(1, n_sp, unroll=True)
    def _(i):
        greet((dp, lax.rem(sp + i, n_sp)))

    @pl.when(owner)
    def _():
        @pl.loop(1, n_dp)
        def _(i):
            greet((lax.rem(dp + i, n_dp), sp))

    for copy in later:
        copy.start()

    def remote(source, target, send, recv, place):
        return pltpu.make_async_remote_copy(
            src_ref=source, dst_ref=target, send_sem=send, recv_sem=recv, device_id=place, device_id_type=MESH
        )

    def wait_bytes(sem, ref):
        pltpu.make_async_copy(ref, ref, sem).wait()

    def to_spatial(box, index):
        @pl.loop(1, n_sp, unroll=True)
        def _(i):
            there = lax.rem(sp + i, n_sp)
            remote(box.at[sp], box.at[sp], send_sem.at[index], recv_sem.at[index], (dp, there)).start()

    def to_owners(source_of, box, index):
        for j in range(2):
            there = 2 * sp + j

            @pl.when(there != dp)
            def _():
                remote(source_of(j), box.at[dp], send_sem.at[index], recv_sem.at[index], (there, sp)).start()

    def sent_to_owners(box, index):
        @pl.when(owner)
        def _():
            wait_bytes(send_sem.at[index], box.at[pl.ds(0, 1)])

        @pl.when(jnp.logical_not(owner))
        def _():
            wait_bytes(send_sem.at[index], box.at[pl.ds(0, 2)])

    def from_owner(ref, index):
        @pl.loop(1, n_sp, unroll=True)
        def _(i):
            there = lax.rem(sp + i, n_sp)
            remote(ref, ref, send_sem.at[index], recv_sem.at[index], (dp, there)).start()

    def others(box):
        return box.at[pl.ds(0, box.shape[0] - 1)]

    def receive(box, index):
        wait_bytes(recv_sem.at[index], others(box))

    def total(box):
        return jnp.sum(box[...], axis=0)

    vocab = table.shape[0]
    batch, tokens = ids_ref.shape
    loads[0].wait()
    local_ids = ids_ref[...] - (dp * n_sp + sp) * vocab
    rows_of_vocab = iota((vocab, tokens), 0)
    matches = jnp.concatenate(
        [(local_ids[b : b + 1, :] == rows_of_vocab).astype(F32).astype(BF16) for b in range(batch)], axis=1
    )
    every = (batch, batch * tokens)
    sample = 2 * (iota(every, 0) & (n_sp - 1)) + lax.shift_right_logical(iota(every, 0), n_sp.bit_length() - 1)
    member = (lax.shift_right_logical(iota(every, 1), tokens.bit_length() - 1) == sample).astype(F32).astype(BF16)
    counts = dot(member, matches, ((1,), (1,))).astype(BF16)
    loads[1].wait()
    partial = dot(counts, table[...])
    for i in range(8):
        for j in range(2):
            text_out[:, j, i, :] = partial[j * n_sp : (j + 1) * n_sp, i * LANES : (i + 1) * LANES]

    loads[2].wait()
    coarse_f = coarse[...].astype(F32)
    coarse_sums = jnp.concatenate(
        as_rows(jnp.sum(coarse_f, axis=0, keepdims=True))
        + as_rows(jnp.sum(coarse_f * coarse_f, axis=0, keepdims=True)),
        axis=0,
    )
    for i in range(n_sp):
        text_out[i, 2] = coarse_sums

    pl.semaphore_wait(barrier, jnp.where(owner, n_sp, n_sp + 1))

    @pl.loop(1, n_sp, unroll=True)
    def _(i):
        there = lax.rem(sp + i, n_sp)
        remote(text_out.at[there], text_box.at[sp], send_sem.at[TEXT], recv_sem.at[TEXT], (dp, there)).start()

    text_box[sp] = text_out[sp]

    last = pixels - width

    def edges(source, target, first):
        down = remote(
            source.at[pl.ds(last, width)], target.at[0], edge_send.at[first], edge_recv.at[first], (dp, sp + 1)
        )
        upward = remote(
            source.at[pl.ds(0, width)], target.at[1], edge_send.at[first + 1], edge_recv.at[first + 1], (dp, sp - 1)
        )
        return down, upward

    def start_edges(source, target, first):
        down, upward = edges(source, target, first)

        @pl.when(sp < n_sp - 1)
        def _():
            down.start()

        @pl.when(sp > 0)
        def _():
            upward.start()

    def receive_edges(source, target, first):
        down, upward = edges(source, target, first)

        @pl.when(sp > 0)
        def _():
            down.wait_recv()

        @pl.when(sp < n_sp - 1)
        def _():
            upward.wait_recv()

        @pl.when(sp == 0)
        def _():
            target[0] = jnp.zeros((width, channels), BF16)

        @pl.when(sp == n_sp - 1)
        def _():
            target[1] = jnp.zeros((width, channels), BF16)

    def finish_edges(source, target, first):
        down, upward = edges(source, target, first)

        @pl.when(sp < n_sp - 1)
        def _():
            down.wait_send()

        @pl.when(sp > 0)
        def _():
            upward.wait_send()

    loads[3].wait()
    start_edges(cot, cot_edge, 0)
    pair_cot = remote(
        cot.at[:, other_lanes], cot_chip.at[own_rows], send_sem.at[PAIR_COT], recv_sem.at[PAIR_COT], (dp, other_sp)
    )
    pair_cot.start()
    far = remote(
        cot.at[pl.ds(pl.multiple_of(core * last, width), width), own_lanes],
        far_edge,
        send_sem.at[FAR],
        recv_sem.at[FAR],
        (dp, sp - 2 + 4 * core),
    )
    chips = n_sp // 2
    sends_far = jnp.logical_or(jnp.logical_and(core == 0, chip > 0), jnp.logical_and(core == 1, chip < chips - 1))
    takes_far = jnp.logical_or(jnp.logical_and(core == 0, chip < chips - 1), jnp.logical_and(core == 1, chip > 0))

    @pl.when(sends_far)
    def _():
        far.start()

    for copy in stacks:
        copy.start()

    shape = chosen.shape
    coarse_cols = width // 4
    place = iota(shape, 0)
    wanted = lax.shift_right_logical(place, width.bit_length() - 1) * coarse_cols + (
        lax.shift_right_logical(place & (width - 1), 2)
    )
    chosen[...] = (wanted == iota(shape, 1)).astype(F32).astype(BF16)

    def turn_rows(first_row):
        @pl.loop(0, tile_rows, unroll=True)
        def _(r):
            start = pl.multiple_of(first_row + r * width, width)
            turned_shifts(cot_chip[pl.ds(start, width), :].astype(F32), cot_turned, start)

    loads[4].wait()
    turn_rows(width + own_pixels)

    receive(text_box, TEXT)
    first_sums = total(text_box)
    text_sum[...] = first_sums[0:2]
    to_owners(lambda j: text_sum.at[j], text_dp_box, TEXT_DP)

    later[1].wait()
    coarse_total = group_total(first_sums[2], coarse.shape[1] // GROUPS)
    coarse_count = coarse.shape[0] * n_sp * (coarse.shape[1] // GROUPS)
    tiles = coarse.shape[1] // LANES
    c_mean = coarse_total[0:tiles, :] / coarse_count
    c_scale = lax.rsqrt(coarse_total[tiles : 2 * tiles, :] / coarse_count - c_mean * c_mean + EPS)
    c_normed = (coarse[...].astype(F32) - as_row(c_mean, 0, tiles)) * as_row(c_scale, 0, tiles)
    coarse_act = (c_normed * sigmoid(c_normed)).astype(BF16)
    skip = dot(coarse_act, w_skip[...]).astype(BF16)
    up[...] = dot(chosen[...], skip)

    later[0].wait()

    def merge(r, sums):
        start = pl.multiple_of(r * width, width)
        up_start = pl.multiple_of((r // 4) * width, width)
        rows = (feat[pl.ds(start, width), :].astype(F32) + up[pl.ds(up_start, width), :]).astype(BF16)
        merged[pl.ds(start, width), :] = rows
        rows = rows.astype(F32)
        first, second = sums
        first = first + jnp.sum(rows.reshape(width // 8, 8, channels), axis=0)
        second = second + jnp.sum((rows * rows).reshape(width // 8, 8, channels), axis=0)
        return first, second

    zero = jnp.zeros((8, channels), F32)
    first, second = lax.fori_loop(0, tile_rows, merge, (zero, zero), unroll=True)

    def sums_tile(one, two):
        one = jnp.sum(one, axis=0, keepdims=True)
        two = jnp.sum(two, axis=0, keepdims=True)
        return jnp.concatenate(as_rows(one) + as_rows(two) + [jnp.zeros((4, LANES), F32)], axis=0)

    fine_box[sp] = sums_tile(first, second)
    to_spatial(fine_box, FINE)

    @pl.when(owner)
    def _():
        text_dp_box[dp] = text_sum[dp % 2]
        receive(text_dp_box, TEXT_DP)
        pooled[...] = total(text_dp_box)
        from_owner(pooled, POOLED)

    wait_bytes(recv_sem.at[PAIR_COT], cot_chip.at[own_rows])
    turn_rows(width + other_pixels)
    receive_edges(cot, cot_edge, 0)

    @pl.when(takes_far)
    def _():
        far.wait_recv()

    @pl.when(jnp.logical_not(takes_far))
    def _():
        far_edge[...] = jnp.zeros((width, half), BF16)

    near = cot_edge[core, :, own_lanes].astype(F32)
    farther = far_edge[...].astype(F32)
    turned_shifts(jnp.where(core == 0, near, farther), cot_turned, 0)
    turned_shifts(jnp.where(core == 0, farther, near), cot_turned, width + 2 * pixels)

    @pl.when(jnp.logical_not(owner))
    def _():
        wait_bytes(recv_sem.at[POOLED], pooled)

    row, lane = iota((8, LANES), 0), iota((8, LANES), 1)
    half_width = 4 * LANES
    index = ((row & 3) * LANES + lane).astype(F32)
    angle = time_ref[0].astype(F32) * jnp.exp(-math.log(10000.0) * index / half_width)
    embed = jnp.where(row < 4, jnp.sin(angle), jnp.cos(angle)) + pooled[...] / tokens
    embed = (embed * sigmoid(embed)).astype(BF16).astype(F32)
    mod_out[8:16, :] = embed
    later[2].wait()
    embed_row = jnp.broadcast_to(as_row(embed, 0, 8), (8, 8 * LANES)).astype(BF16)
    modulation = dot(embed_row, w_mod[...])[0:1, :]
    gain = 1.0 + modulation[:, :channels]
    shift = modulation[:, channels:]

    receive(fine_box, FINE)
    fine_total = group_total(total(fine_box), channels // GROUPS)
    fine_count = pixels * n_sp * (channels // GROUPS)
    f_mean = fine_total[0:2, :] / fine_count
    f_scale = lax.rsqrt(fine_total[2:4, :] / fine_count - f_mean * f_mean + EPS)
    center, scale = as_row(f_mean, 0, 2), as_row(f_scale, 0, 2)

    @pl.loop(0, tile_rows, unroll=True)
    def _(r):
        start = pl.multiple_of(r * width, width)
        pre = (merged[pl.ds(start, width), :].astype(F32) - center) * scale * gain + shift
        act = pre * sigmoid(pre)
        hidden[pl.ds(start, width), :] = act.astype(BF16)
        low, high = act[:, :half], act[:, half:]
        block = lax.shift_right_logical(iota(low.shape, 1), 5)
        even = jnp.where((block & 1) == 0, low, pltpu.roll(high, 32, 1))
        odd = jnp.where((block & 1) == 0, pltpu.roll(low, LANES - 32, 1), high)
        rows = pl.ds(pl.multiple_of(own_pixels + start, width), width)
        hidden_pair[rows, :] = jnp.concatenate([even, odd], axis=1).astype(BF16)

        @pl.when(r % 2 == 1)
        def _():
            two = pl.ds(pl.multiple_of(own_pixels + start - width, width), 2 * width)
            remote(
                hidden_pair.at[two], hidden_pair.at[two], send_sem.at[PAIR_HIDDEN], recv_sem.at[PAIR_HIDDEN], (dp, other_sp)
            ).start()

    def weight_term(dr, first_pixel):
        lanes = pl.ds(pl.multiple_of((2 - dr) * width + first_pixel, width), pixels)
        return dot(cot_turned[:, lanes], hidden_pair[pl.ds(first_pixel, pixels), :])

    for dr in range(3):
        weight_own[dr] = weight_term(dr, own_pixels)
    wait_bytes(recv_sem.at[PAIR_HIDDEN], hidden_pair.at[pl.ds(0, pixels)])
    for dr in range(3):
        grads = weight_own[dr] + weight_term(dr, other_pixels)
        for dc in range(3):
            tap = 3 * dr + dc
            grad = grads[dc * half : (dc + 1) * half, :]
            if tap < 8:
                cube_out[tap % 2, tap // 2, 0, 0:half] = grad[:, :half].astype(BF16)
                cube_out[tap % 2, tap // 2, 1, 0:half] = grad[:, half:].astype(BF16)
            else:
                turned = grad.T.astype(BF16)
                for side in range(2):
                    for number in range(8):
                        first = (number % 2) * half + block_of(number // 2) * 32 + side * 16
                        cube_out[side, number // 2, number % 2, half : half + 16] = turned[first : first + 16, :]

    for side in range(2):
        for d in range(1, 8):
            dx, dy, dz = d % 2, (d // 2) % 2, d // 4
            their_quarter = 2 * (odd_z + dz - 2 * odd_z * dz) + (odd_x + dx - 2 * odd_x * dx)
            their_y = odd_y + dy - 2 * odd_y * dy
            remote(
                cube_out.at[side, their_quarter, their_y],
                cube_box.at[side, d],
                send_sem.at[CUBE + side],
                recv_sem.at[CUBE + side],
                neighbour(side, d),
            ).start()
    for side in range(2):
        cube_box[side, 0] = cube_out[side, quarter, odd_y]

    start_edges(hidden, hid_edge, 2)

    @pl.loop(0, tile_rows, unroll=True)
    def _(r):
        start = pl.multiple_of(r * width, width)
        column_shifts(cot[pl.ds(start, width), :].astype(F32), cot_spread, pl.multiple_of(start + width, width), True)

    column_shifts(cot_edge[0].astype(F32), cot_spread, 0, True)
    column_shifts(cot_edge[1].astype(F32), cot_spread, pixels + width, True)
    later[3].wait()
    chunk = pixels // 2

    @pl.loop(0, 2)
    def _(c):
        start = pl.multiple_of(c * chunk, chunk)
        grad = None
        for dr in range(3):
            term = dot(
                cot_spread[pl.ds(pl.multiple_of(start + (2 - dr) * width, width), chunk), :],
                w_conv[:, 3 * dr * channels : 3 * (dr + 1) * channels],
                ((1,), (1,)),
            )
            grad = term if grad is None else grad + term
        grad_hid[pl.ds(start, chunk), :] = grad

    def backward(r, sums):
        start = pl.multiple_of(r * width, width)
        normed = (merged[pl.ds(start, width), :].astype(F32) - center) * scale
        pre = normed * gain + shift
        sigma = sigmoid(pre)
        grad = grad_hid[pl.ds(start, width), :] * sigma * (1.0 + pre * (1.0 - sigma))
        grad_hid[pl.ds(start, width), :] = grad
        first, second = sums
        first = first + jnp.sum((grad * normed).reshape(width // 8, 8, channels), axis=0)
        second = second + jnp.sum(grad.reshape(width // 8, 8, channels), axis=0)
        return first, second

    first, second = lax.fori_loop(0, tile_rows, backward, (zero, zero), unroll=True)
    back_box[sp] = sums_tile(first, second)
    to_spatial(back_box, BACK)

    for side in range(2):
        wait_bytes(recv_sem.at[CUBE + side], cube_box.at[side, pl.ds(1, 7)])
        summed = cube_box[side, 0].astype(F32)
        for d in range(1, 8):
            summed = summed + cube_box[side, d].astype(F32)
        weight_sum[side] = summed[0:half, :].T
        tail_sum[side * 16 : (side + 1) * 16, :] = summed[half : half + 16, :]

    def part_of(number):
        rows = block_of((number // 4) % 4) * 32 + (number % 4) * part
        return weight_sum.at[number // 16, pl.ds(pl.multiple_of(rows, part), part)]

    @pl.loop(1, n_dp, unroll=True)
    def _(i):
        number = lax.rem(rank + i, n_dp)
        remote(part_of(number), tile_box.at[rank], send_sem.at[TILE], recv_sem.at[TILE], of_rank(number)).start()

    for m in range(4):
        number = quarter * 4 + m

        @pl.when(number != rank)
        def _():
            remote(
                tail_sum.at[pl.ds(m * part, part)],
                tail_box.at[rank],
                send_sem.at[TAIL],
                recv_sem.at[TAIL],
                of_rank(number),
            ).start()

        @pl.when(number == rank)
        def _():
            tail_box[rank] = tail_sum[m * part : (m + 1) * part, :]

    tile_box[rank] = part_of(rank)[...]

    @pl.loop(0, tile_rows, unroll=True)
    def _(r):
        start = pl.multiple_of(r * width, width)
        column_shifts(hidden[pl.ds(start, width), :].astype(F32), hid_spread, pl.multiple_of(start + width, width), False)

    receive_edges(hidden, hid_edge, 2)
    column_shifts(hid_edge[0].astype(F32), hid_spread, 0, False)
    column_shifts(hid_edge[1].astype(F32), hid_spread, pixels + width, False)
    for copy in stacks:
        copy.wait()

    @pl.loop(0, 2)
    def _(c):
        start = pl.multiple_of(c * chunk, chunk)
        conv = merged[pl.ds(start, chunk), :].astype(F32)
        for dr in range(3):
            conv = conv + dot(
                hid_spread[pl.ds(pl.multiple_of(start + dr * width, width), chunk), :],
                w_stack[3 * dr * channels : 3 * (dr + 1) * channels, :],
            )
        out_ref[pl.ds(start, chunk), :] = conv.astype(BF16)

    stores = [
        pltpu.make_async_copy(source, target, store_sem.at[i])
        for i, (source, target) in enumerate(
            (
                (out_ref, out_hbm), (grad_feat_ref, grad_feat_hbm),
                (grad_mod_ref, grad_mod_hbm), (grad_conv_ref, grad_conv_hbm),
            )
        )
    ]
    stores[0].start()

    receive(back_box, BACK)
    back = total(back_box)
    mod_out[0:8, :] = back
    to_owners(lambda j: mod_out, mod_box, MOD)
    gain_tile = jnp.concatenate(as_rows(gain) + as_rows(gain), axis=0)
    means = group_total(back[0:4, :] * gain_tile, channels // GROUPS) / fine_count
    mean_two, mean_one = as_row(means, 0, 2), as_row(means, 2, 2)

    @pl.loop(0, tile_rows, unroll=True)
    def _(r):
        start = pl.multiple_of(r * width, width)
        normed = (merged[pl.ds(start, width), :].astype(F32) - center) * scale
        inner = grad_hid[pl.ds(start, width), :] * gain - mean_one - normed * mean_two
        grad_feat_ref[pl.ds(start, width), :] = (cot[pl.ds(start, width), :].astype(F32) + scale * inner).astype(BF16)

    stores[1].start()

    receive(tile_box, TILE)
    final_box[sp] = total(tile_box)
    to_spatial(final_box, FINAL)

    @pl.when(owns_tail)
    def _():
        receive(tail_box, TAIL)
        final_tail_box[core] = total(tail_box)

        @pl.loop(1, n_sp)
        def _(i):
            there = lax.rem(sp + i, n_sp)
            remote(
                final_tail_box.at[core], final_tail_box.at[core], send_sem.at[FINAL_TAIL], recv_sem.at[FINAL_TAIL], (dp, there)
            ).start()

    @pl.when(owner)
    def _():
        mod_box[dp] = mod_out[...]
        receive(mod_box, MOD)
        share = 8 * LANES // n_dp
        in_lanes = LANES // share
        row_of_share = dp // in_lanes
        embeds = jnp.sum(
            jnp.where(iota((n_dp, 8, LANES), 1) == row_of_share, mod_box[:, 8:16, :], 0.0), axis=1
        ).astype(BF16)
        rest = jnp.concatenate([mod_box[:, i, :] for i in range(4)], axis=1)
        grads = None
        for _ in range(3):
            piece = rest.astype(BF16)
            rest = rest - piece.astype(F32)
            term = dot(embeds, piece, ((0,), (0,)))
            grads = term if grads is None else grads + term
        mod_rows[...] = grads
        mod_start = pl.multiple_of((dp % in_lanes) * share, share)
        grad_mod_ref[...] = mod_rows[pl.ds(mod_start, share), :].astype(BF16)
        from_owner(grad_mod_ref, GRAD_MOD)

    @pl.when(jnp.logical_not(owner))
    def _():
        wait_bytes(recv_sem.at[GRAD_MOD], grad_mod_ref)

    stores[2].start()

    receive(final_box, FINAL)

    @pl.when(owns_tail)
    def _():
        wait_bytes(recv_sem.at[FINAL_TAIL], final_tail_box.at[0])

    @pl.when(jnp.logical_not(owns_tail))
    def _():
        wait_bytes(recv_sem.at[FINAL_TAIL], final_tail_box)

    holders = [
        8 * (tap // 4) + 2 * (2 * (tap % 2) + (tap // 2) % 2) + side for tap in range(8) for side in range(2)
    ]
    grad_conv_ref[...] = jnp.concatenate(
        [final_box[j] for j in holders] + [final_tail_box[0], final_tail_box[1]], axis=1
    ).astype(BF16)

    stores[3].start()

    for box, index in (
        (fine_box, FINE), (back_box, BACK), (text_box, TEXT), (tile_box, TILE),
        (final_box, FINAL),
    ):
        wait_bytes(send_sem.at[index], others(box))

    for side in range(2):
        wait_bytes(send_sem.at[CUBE + side], cube_box.at[side, pl.ds(1, 7)])
    sent_to_owners(text_dp_box, TEXT_DP)
    sent_to_owners(mod_box, MOD)

    @pl.when(owner)
    def _():
        wait_bytes(send_sem.at[POOLED], final_box.at[pl.ds(0, n_sp - 1)])
        rows = (n_sp - 1) * grad_mod_ref.shape[0] * 2
        wait_bytes(send_sem.at[GRAD_MOD], hidden.at[pl.ds(0, rows)])

    pair_cot.wait_send()
    wait_bytes(send_sem.at[PAIR_HIDDEN], hidden_pair.at[pl.ds(0, pixels)])

    @pl.when(sends_far)
    def _():
        far.wait_send()

    finish_edges(cot, cot_edge, 0)
    finish_edges(hidden, hid_edge, 2)

    @pl.when(owns_tail)
    def _():
        wait_bytes(send_sem.at[TAIL], tail_box.at[pl.ds(0, 3)])
        wait_bytes(send_sem.at[FINAL_TAIL], final_box.at[pl.ds(0, n_sp - 1)])

    @pl.when(jnp.logical_not(owns_tail))
    def _():
        wait_bytes(send_sem.at[TAIL], tail_box.at[pl.ds(0, 4)])

    for store in stores:
        store.wait()


def write(*refs):
    sources, targets, rooms, load_sem, store_sem = refs[:4], refs[4:8], refs[8:12], refs[12], refs[13]
    moves = []
    for source, room, target in zip(sources, rooms, targets):
        rows = source.shape[0]
        pieces = 4 if rows >= 1024 else 1
        for i in range(pieces):
            piece = pl.ds(i * rows // pieces, rows // pieces)
            number = len(moves)
            moves.append(
                (
                    pltpu.make_async_copy(source.at[piece], room.at[piece], load_sem.at[number]),
                    pltpu.make_async_copy(room.at[piece], target.at[piece], store_sem.at[number]),
                )
            )
    for fetch, _ in moves:
        fetch.start()
    for fetch, store in moves:
        fetch.wait()
        store.start()
    for _, store in moves:
        store.wait()


def body(n_dp, n_sp, features, coarse, timestep, text_ids, text_table, w_mod, w_skip, w_conv, cotangent):
    _, tile_rows, width, channels = features.shape
    pixels = tile_rows * width
    cells = coarse.shape[1] * coarse.shape[2]
    coarse_width = coarse.shape[3]
    part, half = channels // n_dp, channels // 2
    taps = w_conv.shape[1] // channels
    vm = pltpu.VMEM
    tile = (8, LANES)
    anywhere = pl.BlockSpec(memory_space=pl.ANY)
    mod_rows = w_mod.shape[0] // n_dp
    scratch = [
        vm((pixels, channels), BF16),
        vm((pixels, channels), BF16),
        vm((part, taps * channels), BF16),
        vm((mod_rows, 2 * channels), BF16),
        vm(text_ids.shape, jnp.int32),
        vm((pixels, channels), BF16),
        vm((cells, coarse_width), BF16),
        vm(text_table.shape, BF16),
        vm(w_mod.shape, BF16),
        vm(w_skip.shape, BF16),
        vm(w_conv.shape, BF16),
        vm((taps * channels, channels), BF16),
        vm((pixels, channels), BF16),
        vm((2, width, channels), BF16),
        vm((width, half), BF16),
        vm((2, width, channels), BF16),
        vm((2 * pixels + 2 * width, half), BF16),
        vm((pixels + 2 * width, 3 * channels), BF16),
        vm((3 * half, 2 * pixels + 2 * width), BF16),
        vm((pixels + 2 * width, 3 * channels), BF16),
        vm((4 * cells, cells), BF16),
        vm((4 * cells, channels), F32),
        vm((pixels, channels), BF16),
        vm((pixels, channels), BF16),
        vm((2 * pixels, channels), BF16),
        vm((pixels, channels), F32),
        vm((n_sp,) + tile, F32),
        vm((n_sp,) + tile, F32),
        vm((n_sp, 3) + tile, F32),
        vm((n_sp, 3) + tile, F32),
        vm((2,) + tile, F32),
        vm((n_dp,) + tile, F32),
        vm(tile, F32),
        vm((16, LANES), F32),
        vm((n_dp, 16, LANES), F32),
        vm((LANES, 2 * channels), F32),
        vm((3, 3 * half, channels), F32),
        vm((2, 4, 2, half + 16, half), BF16),
        vm((2, 8, half + 16, half), BF16),
        vm((2, half, half), F32),
        vm((32, half), F32),
        vm((n_dp, part, half), F32),
        vm((n_dp, part, half), F32),
        vm((n_sp, part, half), F32),
        vm((2, part, half), F32),
        pltpu.SemaphoreType.DMA((9 + taps,)),
        pltpu.SemaphoreType.DMA((4,)),
        pltpu.SemaphoreType.DMA((4,)),
        pltpu.SemaphoreType.DMA((4,)),
        pltpu.SemaphoreType.DMA((16,)),
        pltpu.SemaphoreType.DMA((16,)),
    ]
    shapes = (
        jax.ShapeDtypeStruct((pixels, channels), BF16),
        jax.ShapeDtypeStruct((pixels, channels), BF16),
        jax.ShapeDtypeStruct((part, taps * channels), BF16),
        jax.ShapeDtypeStruct((mod_rows, 2 * channels), BF16),
    )
    results = pl.pallas_call(
        functools.partial(kernel, n_dp, n_sp, tile_rows, width),
        out_shape=shapes,
        in_specs=[pl.BlockSpec(memory_space=pltpu.SMEM)] + [anywhere] * 8,
        out_specs=(anywhere,) * 4,
        scratch_shapes=scratch,
        compiler_params=pltpu.CompilerParams(
            collective_id=0, has_side_effects=True, vmem_limit_bytes=VMEM_LIMIT
        ),
    )(
        timestep,
        text_ids,
        features.reshape(pixels, channels),
        coarse.reshape(cells, coarse_width),
        text_table,
        w_mod,
        w_skip,
        w_conv,
        cotangent.reshape(pixels, channels),
    )
    output, grad_features, grad_conv, grad_mod = pl.pallas_call(
        write,
        out_shape=shapes,
        in_specs=[anywhere] * 4,
        out_specs=(anywhere,) * 4,
        scratch_shapes=[vm(shape.shape, shape.dtype) for shape in shapes]
        + [pltpu.SemaphoreType.DMA((10,)), pltpu.SemaphoreType.DMA((10,))],
        compiler_params=pltpu.CompilerParams(vmem_limit_bytes=VMEM_LIMIT),
    )(*results)
    return output.reshape(features.shape), grad_features.reshape(features.shape), grad_conv, grad_mod


def solution(mesh):
    in_specs = (
        P("dp", "spatial", None, None),
        P("dp", "spatial", None, None),
        P("dp"),
        P(),
        P(("dp", "spatial"), None),
        P(),
        P(),
        P(),
        P("dp", "spatial", None, None),
    )
    out_specs = (
        P("dp", "spatial", None, None),
        P("dp", "spatial", None, None),
        P("dp", None),
        P("dp", None),
    )
    step = functools.partial(body, mesh.shape["dp"], mesh.shape["spatial"])
    return jax.shard_map(step, mesh=mesh, in_specs=in_specs, out_specs=out_specs, check_vma=False)
```

time: 691 us -> 60 us (0.09)
  the two profiles are of different devices: /device:TPU:32 before, /device:TPU:71 now
where the time goes in v1:
time: 60 us; the launch traced here: 59.9 us
  Pallas kernels  58.6 us (98%)
  between operations  1.29 us (2%)
    pallas_call x1, Pallas kernels, body(): pl.pallas_call(functools.partial(kernel, n_dp, n_sp, tile_rows, width), o...  56.4 us
    pallas_call x1, Pallas kernels, body(): pl.pallas_call(write, out_shape=shapes, in_specs=[anywhere] * 4, out_spec...  2.14 us

profile of v1, /device:TPU:71, one launch (start us, length us, event | category | flops | bytes accessed | tf_op | source)
XLA Modules:
  0.0 59.9 jit_solution(3264719112360256059)
XLA Ops:
  1.3 56.4 %shard_map.120 = (bf16[1024,256]{1,0:T(8,128)(2,1)}, bf16[1024,256]{1,0:T(8,128)(2,1)}, bf16[8,2304]{1,0:T(8,128)(2,1)}, bf16[32,512]{1,0:T(8,128)(2,1)}) custom-call(s32[1]{0:T(128)S(6)} %copy.13.refs_0_, s32[32,128]{1,0:T(8,128)} %refs_1_.1, bf16[1024,256]{1,0:T(8,128)(2,1)} %bitcast.5, bf16[64,512]{1,0:T(8,128)(2,1)} %bitcast.7, ...), custom_call_target="tpu_custom_call" | custom-call | tf_op jit(solution)/shard_map/pallas_call | solution.py:819
  57.7 2.1 %shard_map.121 = (bf16[1024,256]{1,0:T(8,128)(2,1)}, bf16[1024,256]{1,0:T(8,128)(2,1)}, bf16[8,2304]{1,0:T(8,128)(2,1)}, bf16[32,512]{1,0:T(8,128)(2,1)}) custom-call(bf16[1024,256]{1,0:T(8,128)(2,1)} %get-tuple-element.12.refs_0_, bf16[1024,256]{1,0:T(8,128)(2,1)} %get-tuple-element.13.refs_1_, bf16[8,2304]{1,0:T(8,128)(2,1)} %get-tuple-element.14.refs_2_, ...), custom_call_target="tpu_custom_call" | custom-call | tf_op jit(solution)/shard_map/pallas_call | solution.py:839

commit v2 on v1

--- a/solution.py
+++ b/solution.py
@@ -76,11 +76,11 @@
         out_hbm, grad_feat_hbm, grad_conv_hbm, grad_mod_hbm,
         out_ref, grad_feat_ref, grad_conv_ref, grad_mod_ref, ids_ref,
         feat, coarse, table, w_mod, w_skip, w_conv, w_stack, cot,
-        cot_edge, far_edge, hid_edge, cot_chip, cot_spread, cot_turned, hid_spread, chosen, up, merged,
+        cot_edge, far_edge, hid_edge, cot_half, cot_chip, cot_spread, cot_turned, hid_spread, chosen, up, merged,
         hidden, hidden_pair, grad_hid,
-        fine_box, back_box, text_out, text_box, text_sum, text_dp_box, pooled, mod_out, mod_box, mod_rows,
+        fine_box, back_box, text_out, text_box, text_sum, text_dp_box, pooled, mod_out, mod_box, mod_rows, grad_mod_parts,
         weight_own, cube_out, cube_box, weight_sum, tail_sum,
-        tile_box, tail_box, final_box, final_tail_box,
+        tile_box, tail_box, final_box,
         load_sem, store_sem, edge_send, edge_recv, send_sem, recv_sem,
     ) = refs
     channels = feat.shape[1]
@@ -116,10 +116,12 @@
 
     owns_tail = jnp.logical_and(high_y == quarter, high_x == 0)
     owner = dp // 2 == sp
+    from_first = lax.rem(sp - dp // 2 + n_sp, n_sp)
+    quarter_owner = from_first % 4 == 0
     (
-        FINE, BACK, TEXT, TEXT_DP, POOLED, MOD, GRAD_MOD, TILE, TAIL, FINAL, FINAL_TAIL,
+        FINE, BACK, TEXT, TEXT_DP, POOLED, MOD, GRAD_MOD, TILE, TAIL, FINAL,
         PAIR_COT, PAIR_HIDDEN, FAR, CUBE,
-    ) = range(15)
+    ) = range(14)
 
     def load(source, target, index):
         return pltpu.make_async_copy(source, target, load_sem.at[index])
@@ -134,21 +136,12 @@
         load(table_hbm, table, 2),
         load(coarse_hbm, coarse, 0),
         load(cot_hbm, cot, 3),
-        load(cot_hbm.at[:, own_lanes], cot_chip.at[own_rows], 4),
     ]
     later = [
-        load(feat_hbm, feat, 5),
-        load(w_skip_hbm, w_skip, 6),
-        load(w_mod_hbm, w_mod, 7),
-        load(w_conv_hbm, w_conv, 8),
-    ]
-    stacks = [
-        load(
-            w_conv_hbm.at[:, pl.ds(tap * channels, channels)],
-            w_stack.at[pl.ds(tap * channels, channels), :],
-            9 + tap,
-        )
-        for tap in range(9)
+        load(feat_hbm, feat, 4),
+        load(w_skip_hbm, w_skip, 5),
+        load(w_mod_hbm, w_mod, 6),
+        load(w_conv_hbm, w_conv, 7),
     ]
     for copy in loads:
         copy.start()
@@ -308,12 +301,14 @@
 
     loads[3].wait()
     start_edges(cot, cot_edge, 0)
+    cot_half[...] = cot[:, other_lanes]
+    cot_chip[own_rows, :] = cot[:, own_lanes]
     pair_cot = remote(
-        cot.at[:, other_lanes], cot_chip.at[own_rows], send_sem.at[PAIR_COT], recv_sem.at[PAIR_COT], (dp, other_sp)
+        cot_half, cot_chip.at[own_rows], send_sem.at[PAIR_COT], recv_sem.at[PAIR_COT], (dp, other_sp)
     )
     pair_cot.start()
     far = remote(
-        cot.at[pl.ds(pl.multiple_of(core * last, width), width), own_lanes],
+        cot_chip.at[pl.ds(pl.multiple_of(width + core * (pixels + last), width), width)],
         far_edge,
         send_sem.at[FAR],
         recv_sem.at[FAR],
@@ -327,9 +322,6 @@
     def _():
         far.start()
 
-    for copy in stacks:
-        copy.start()
-
     shape = chosen.shape
     coarse_cols = width // 4
     place = iota(shape, 0)
@@ -344,7 +336,6 @@
             start = pl.multiple_of(first_row + r * width, width)
             turned_shifts(cot_chip[pl.ds(start, width), :].astype(F32), cot_turned, start)
 
-    loads[4].wait()
     turn_rows(width + own_pixels)
 
     receive(text_box, TEXT)
@@ -421,7 +412,6 @@
     angle = time_ref[0].astype(F32) * jnp.exp(-math.log(10000.0) * index / half_width)
     embed = jnp.where(row < 4, jnp.sin(angle), jnp.cos(angle)) + pooled[...] / tokens
     embed = (embed * sigmoid(embed)).astype(BF16).astype(F32)
-    mod_out[8:16, :] = embed
     later[2].wait()
     embed_row = jnp.broadcast_to(as_row(embed, 0, 8), (8, 8 * LANES)).astype(BF16)
     modulation = dot(embed_row, w_mod[...])[0:1, :]
@@ -569,16 +559,33 @@
 
     tile_box[rank] = part_of(rank)[...]
 
+    receive(back_box, BACK)
+    back = total(back_box)
+    for i in range(4):
+        pair_there = lax.rem(sp - 4 * i + n_sp, n_sp)
+        wanted_row = jnp.sum(jnp.where(row == pair_there // 2, embed, 0.0), axis=0, keepdims=True)
+        mod_out[i] = jnp.concatenate([back[i : i + 1, :], wanted_row, jnp.zeros((6, LANES), F32)], axis=0)
+        for j in range(2):
+            there = 2 * pair_there + j
+
+            @pl.when(there != dp)
+            def _():
+                remote(mod_out.at[i], mod_box.at[dp], send_sem.at[MOD], recv_sem.at[MOD], (there, sp)).start()
+
+            @pl.when(there == dp)
+            def _():
+                mod_box[dp] = mod_out[i]
+
     @pl.loop(0, tile_rows, unroll=True)
     def _(r):
         start = pl.multiple_of(r * width, width)
         column_shifts(hidden[pl.ds(start, width), :].astype(F32), hid_spread, pl.multiple_of(start + width, width), False)
 
+    for tap in range(9):
+        w_stack[tap * channels : (tap + 1) * channels, :] = w_conv[:, tap * channels : (tap + 1) * channels]
     receive_edges(hidden, hid_edge, 2)
     column_shifts(hid_edge[0].astype(F32), hid_spread, 0, False)
     column_shifts(hid_edge[1].astype(F32), hid_spread, pixels + width, False)
-    for copy in stacks:
-        copy.wait()
 
     @pl.loop(0, 2)
     def _(c):
@@ -602,10 +609,6 @@
     ]
     stores[0].start()
 
-    receive(back_box, BACK)
-    back = total(back_box)
-    mod_out[0:8, :] = back
-    to_owners(lambda j: mod_out, mod_box, MOD)
     gain_tile = jnp.concatenate(as_rows(gain) + as_rows(gain), axis=0)
     means = group_total(back[0:4, :] * gain_tile, channels // GROUPS) / fine_count
     mean_two, mean_one = as_row(means, 0, 2), as_row(means, 2, 2)
@@ -620,32 +623,31 @@
     stores[1].start()
 
     receive(tile_box, TILE)
-    final_box[sp] = total(tile_box)
-    to_spatial(final_box, FINAL)
-
-    @pl.when(owns_tail)
-    def _():
-        receive(tail_box, TAIL)
-        final_tail_box[core] = total(tail_box)
-
-        @pl.loop(1, n_sp)
+    final_box[sp, 0] = total(tile_box)
+
+    def to_group(source):
+        @pl.loop(1, n_sp, unroll=True)
         def _(i):
             there = lax.rem(sp + i, n_sp)
-            remote(
-                final_tail_box.at[core], final_tail_box.at[core], send_sem.at[FINAL_TAIL], recv_sem.at[FINAL_TAIL], (dp, there)
-            ).start()
-
-    @pl.when(owner)
-    def _():
-        mod_box[dp] = mod_out[...]
+            remote(source, source, send_sem.at[FINAL], recv_sem.at[FINAL], (dp, there)).start()
+
+    @pl.when(owns_tail)
+    def _():
+        receive(tail_box, TAIL)
+        final_box[sp, 1] = total(tail_box)
+        to_group(final_box.at[sp])
+
+    @pl.when(jnp.logical_not(owns_tail))
+    def _():
+        to_group(final_box.at[sp, 0])
+
+    @pl.when(quarter_owner)
+    def _():
         receive(mod_box, MOD)
         share = 8 * LANES // n_dp
         in_lanes = LANES // share
-        row_of_share = dp // in_lanes
-        embeds = jnp.sum(
-            jnp.where(iota((n_dp, 8, LANES), 1) == row_of_share, mod_box[:, 8:16, :], 0.0), axis=1
-        ).astype(BF16)
-        rest = jnp.concatenate([mod_box[:, i, :] for i in range(4)], axis=1)
+        embeds = mod_box[:, 1, :].astype(BF16)
+        rest = mod_box[:, 0, :]
         grads = None
         for _ in range(3):
             piece = rest.astype(BF16)
@@ -654,50 +656,61 @@
             grads = term if grads is None else grads + term
         mod_rows[...] = grads
         mod_start = pl.multiple_of((dp % in_lanes) * share, share)
-        grad_mod_ref[...] = mod_rows[pl.ds(mod_start, share), :].astype(BF16)
-        from_owner(grad_mod_ref, GRAD_MOD)
-
-    @pl.when(jnp.logical_not(owner))
-    def _():
-        wait_bytes(recv_sem.at[GRAD_MOD], grad_mod_ref)
-
-    stores[2].start()
-
-    receive(final_box, FINAL)
+        number = from_first // 4
+        grad_mod_parts[number] = mod_rows[pl.ds(mod_start, share), :].astype(BF16)
+        from_owner(grad_mod_parts.at[number], GRAD_MOD)
 
     @pl.when(owns_tail)
     def _():
-        wait_bytes(recv_sem.at[FINAL_TAIL], final_tail_box.at[0])
+        wait_bytes(recv_sem.at[FINAL], tile_box.at[pl.ds(0, n_sp)])
 
     @pl.when(jnp.logical_not(owns_tail))
     def _():
-        wait_bytes(recv_sem.at[FINAL_TAIL], final_tail_box)
+        wait_bytes(recv_sem.at[FINAL], tile_box.at[pl.ds(0, n_sp + 1)])
 
     holders = [
         8 * (tap // 4) + 2 * (2 * (tap % 2) + (tap // 2) % 2) + side for tap in range(8) for side in range(2)
     ]
+    tail_place = (high_y // 2) * 8 + (high_y % 2) * 2
     grad_conv_ref[...] = jnp.concatenate(
-        [final_box[j] for j in holders] + [final_tail_box[0], final_tail_box[1]], axis=1
+        [final_box[j, 0] for j in holders] + [final_box[tail_place, 1], final_box[tail_place + 1, 1]], axis=1
     ).astype(BF16)
 
     stores[3].start()
+
+    @pl.when(quarter_owner)
+    def _():
+        wait_bytes(recv_sem.at[GRAD_MOD], grad_mod_parts.at[pl.ds(0, 3)])
+
+    @pl.when(jnp.logical_not(quarter_owner))
+    def _():
+        wait_bytes(recv_sem.at[GRAD_MOD], grad_mod_parts)
+
+    grad_mod_ref[...] = jnp.concatenate([grad_mod_parts[i] for i in range(4)], axis=1)
+    stores[2].start()
 
     for box, index in (
         (fine_box, FINE), (back_box, BACK), (text_box, TEXT), (tile_box, TILE),
-        (final_box, FINAL),
     ):
         wait_bytes(send_sem.at[index], others(box))
 
     for side in range(2):
         wait_bytes(send_sem.at[CUBE + side], cube_box.at[side, pl.ds(1, 7)])
     sent_to_owners(text_dp_box, TEXT_DP)
-    sent_to_owners(mod_box, MOD)
+
+    @pl.when(quarter_owner)
+    def _():
+        wait_bytes(send_sem.at[MOD], mod_box.at[pl.ds(0, 7)])
+        rows = (n_sp - 1) * grad_mod_parts.shape[1] // 2
+        wait_bytes(send_sem.at[GRAD_MOD], hidden.at[pl.ds(0, rows)])
+
+    @pl.when(jnp.logical_not(quarter_owner))
+    def _():
+        wait_bytes(send_sem.at[MOD], mod_box.at[pl.ds(0, 8)])
 
     @pl.when(owner)
     def _():
-        wait_bytes(send_sem.at[POOLED], final_box.at[pl.ds(0, n_sp - 1)])
-        rows = (n_sp - 1) * grad_mod_ref.shape[0] * 2
-        wait_bytes(send_sem.at[GRAD_MOD], hidden.at[pl.ds(0, rows)])
+        wait_bytes(send_sem.at[POOLED], fine_box.at[pl.ds(0, n_sp - 1)])
 
     pair_cot.wait_send()
     wait_bytes(send_sem.at[PAIR_HIDDEN], hidden_pair.at[pl.ds(0, pixels)])
@@ -712,11 +725,12 @@
     @pl.when(owns_tail)
     def _():
         wait_bytes(send_sem.at[TAIL], tail_box.at[pl.ds(0, 3)])
-        wait_bytes(send_sem.at[FINAL_TAIL], final_box.at[pl.ds(0, n_sp - 1)])
+        wait_bytes(send_sem.at[FINAL], tile_box.at[pl.ds(0, 2 * (n_sp - 1))])
 
     @pl.when(jnp.logical_not(owns_tail))
     def _():
         wait_bytes(send_sem.at[TAIL], tail_box.at[pl.ds(0, 4)])
+        wait_bytes(send_sem.at[FINAL], tile_box.at[pl.ds(0, n_sp - 1)])
 
     for store in stores:
         store.wait()
@@ -774,6 +788,7 @@
         vm((2, width, channels), BF16),
         vm((width, half), BF16),
         vm((2, width, channels), BF16),
+        vm((pixels, half), BF16),
         vm((2 * pixels + 2 * width, half), BF16),
         vm((pixels + 2 * width, 3 * channels), BF16),
         vm((3 * half, 2 * pixels + 2 * width), BF16),
@@ -791,9 +806,10 @@
         vm((2,) + tile, F32),
         vm((n_dp,) + tile, F32),
         vm(tile, F32),
-        vm((16, LANES), F32),
-        vm((n_dp, 16, LANES), F32),
-        vm((LANES, 2 * channels), F32),
+        vm((4,) + tile, F32),
+        vm((n_dp,) + tile, F32),
+        vm((LANES, LANES), F32),
+        vm((4, mod_rows, LANES), BF16),
         vm((3, 3 * half, channels), F32),
         vm((2, 4, 2, half + 16, half), BF16),
         vm((2, 8, half + 16, half), BF16),
@@ -801,14 +817,13 @@
         vm((32, half), F32),
         vm((n_dp, part, half), F32),
         vm((n_dp, part, half), F32),
-        vm((n_sp, part, half), F32),
-        vm((2, part, half), F32),
-        pltpu.SemaphoreType.DMA((9 + taps,)),
+        vm((n_sp, 2, part, half), F32),
+        pltpu.SemaphoreType.DMA((8,)),
         pltpu.SemaphoreType.DMA((4,)),
         pltpu.SemaphoreType.DMA((4,)),
         pltpu.SemaphoreType.DMA((4,)),
-        pltpu.SemaphoreType.DMA((16,)),
-        pltpu.SemaphoreType.DMA((16,)),
+        pltpu.SemaphoreType.DMA((15,)),
+        pltpu.SemaphoreType.DMA((15,)),
     ]
     shapes = (
         jax.ShapeDtypeStruct((pixels, channels), BF16),

time: 60 us -> 59.8 us (level)
  the two profiles are of different devices: /device:TPU:71 before, /device:TPU:1 now
where the time goes in v2:
time: 59.8 us; the launch traced here: 59.6 us
  Pallas kernels  58.3 us (97%)
  between operations  1.29 us (2%)
    pallas_call x1, Pallas kernels, body(): pl.pallas_call(functools.partial(kernel, n_dp, n_sp, tile_rows, width), o...  56.2 us
    pallas_call x1, Pallas kernels, body(): pl.pallas_call(write, out_shape=shapes, in_specs=[anywhere] * 4, out_spec...  2.14 us

profile of v2, /device:TPU:1, one launch (start us, length us, event | category | flops | bytes accessed | tf_op | source)
XLA Modules:
  0.0 59.6 jit_solution(7036430501226028153)
XLA Ops:
  1.3 56.2 %shard_map.120 = (bf16[1024,256]{1,0:T(8,128)(2,1)}, bf16[1024,256]{1,0:T(8,128)(2,1)}, bf16[8,2304]{1,0:T(8,128)(2,1)}, bf16[32,512]{1,0:T(8,128)(2,1)}) custom-call(s32[1]{0:T(128)S(6)} %copy.13.refs_0_, s32[32,128]{1,0:T(8,128)} %refs_1_.1, bf16[1024,256]{1,0:T(8,128)(2,1)} %bitcast.5, bf16[64,512]{1,0:T(8,128)(2,1)} %bitcast.7, ...), custom_call_target="tpu_custom_call" | custom-call | tf_op jit(solution)/shard_map/pallas_call | solution.py:834
  57.5 2.1 %shard_map.121 = (bf16[1024,256]{1,0:T(8,128)(2,1)}, bf16[1024,256]{1,0:T(8,128)(2,1)}, bf16[8,2304]{1,0:T(8,128)(2,1)}, bf16[32,512]{1,0:T(8,128)(2,1)}) custom-call(bf16[1024,256]{1,0:T(8,128)(2,1)} %get-tuple-element.12.refs_0_, bf16[1024,256]{1,0:T(8,128)(2,1)} %get-tuple-element.13.refs_1_, bf16[8,2304]{1,0:T(8,128)(2,1)} %get-tuple-element.14.refs_2_, ...), custom_call_target="tpu_custom_call" | custom-call | tf_op jit(solution)/shard_map/pallas_call | solution.py:854

commit v3 on v2

--- a/solution.py
+++ b/solution.py
@@ -73,14 +73,14 @@
 def kernel(n_dp, n_sp, tile_rows, width, *refs):
     (
         time_ref, ids_hbm, feat_hbm, coarse_hbm, table_hbm, w_mod_hbm, w_skip_hbm, w_conv_hbm, cot_hbm,
-        out_hbm, grad_feat_hbm, grad_conv_hbm, grad_mod_hbm,
-        out_ref, grad_feat_ref, grad_conv_ref, grad_mod_ref, ids_ref,
+        out_hbm, grad_feat_hbm, final_hbm, mod_hbm,
+        out_ref, grad_feat_ref, ids_ref,
         feat, coarse, table, w_mod, w_skip, w_conv, w_stack, cot,
         cot_edge, far_edge, hid_edge, cot_half, cot_chip, cot_spread, cot_turned, hid_spread, chosen, up, merged,
         hidden, hidden_pair, grad_hid,
-        fine_box, back_box, text_out, text_box, text_sum, text_dp_box, pooled, mod_out, mod_box, mod_rows, grad_mod_parts,
-        weight_own, cube_out, cube_box, weight_sum, tail_sum,
-        tile_box, tail_box, final_box,
+        coarse_box, fine_box, back_box, text_rows, text_out, text_box, text_sum, text_dp_box, pooled,
+        mod_out, mod_box, mod_rows, mod_own, weight_own, cube_out, cube_box, weight_out, tail_sum,
+        tile_box, tail_box, final_own,
         load_sem, store_sem, edge_send, edge_recv, send_sem, recv_sem,
     ) = refs
     channels = feat.shape[1]
@@ -110,18 +110,19 @@
         z_there = (z + dz * (1 - 2 * odd_z) * (1 - 2 * side) + 8) % 8
         return (y_there * 4 + z_there // 2, (z_there % 2) * 8 + x_there * 2 + core)
 
-    def of_rank(number):
-        x_there, y_there, z_there = number // 16, (number // 4) % 4, number % 4
-        return ((2 * y_there + odd_y) * 4 + z_there, z_low * 8 + (2 * x_there + odd_x) * 2 + core)
-
-    owns_tail = jnp.logical_and(high_y == quarter, high_x == 0)
+    def gatherer(number):
+        y_there, z_there = number // 4, number % 4
+        return ((2 * y_there + odd_y) * 4 + z_there, z_low * 8 + (2 * (z_there % 2) + odd_x) * 2 + core)
+
+    gathers = high_x == z_high % 2
+    owns_tail = jnp.logical_and(gathers, high_y == quarter)
     owner = dp // 2 == sp
     from_first = lax.rem(sp - dp // 2 + n_sp, n_sp)
     quarter_owner = from_first % 4 == 0
     (
-        FINE, BACK, TEXT, TEXT_DP, POOLED, MOD, GRAD_MOD, TILE, TAIL, FINAL,
+        COARSE, FINE, BACK, TEXT, TEXT_DP, POOLED, MOD, GRAD_MOD, TILE, TAIL, FINAL,
         PAIR_COT, PAIR_HIDDEN, FAR, CUBE,
-    ) = range(14)
+    ) = range(15)
 
     def load(source, target, index):
         return pltpu.make_async_copy(source, target, load_sem.at[index])
@@ -213,30 +214,32 @@
     vocab = table.shape[0]
     batch, tokens = ids_ref.shape
     loads[0].wait()
-    local_ids = ids_ref[...] - (dp * n_sp + sp) * vocab
-    rows_of_vocab = iota((vocab, tokens), 0)
-    matches = jnp.concatenate(
-        [(local_ids[b : b + 1, :] == rows_of_vocab).astype(F32).astype(BF16) for b in range(batch)], axis=1
-    )
-    every = (batch, batch * tokens)
-    sample = 2 * (iota(every, 0) & (n_sp - 1)) + lax.shift_right_logical(iota(every, 0), n_sp.bit_length() - 1)
-    member = (lax.shift_right_logical(iota(every, 1), tokens.bit_length() - 1) == sample).astype(F32).astype(BF16)
-    counts = dot(member, matches, ((1,), (1,))).astype(BF16)
+    local_ids = jnp.concatenate(
+        [ids_ref[pl.ds(j, n_sp, stride=2), :] for j in range(2)], axis=0
+    ) - (dp * n_sp + sp) * vocab
+    turned_ids = local_ids.astype(F32).T
+    quarters = jnp.concatenate([turned_ids] * 4, axis=1) - 16.0 * lax.shift_right_logical(
+        iota((tokens, LANES), 1), 5
+    ).astype(F32)
+    found = [
+        jnp.sum(jnp.where(quarters == float(k), 1.0, 0.0), axis=0, keepdims=True) for k in range(16)
+    ]
+    found = jnp.concatenate(found, axis=0)
+    counts = jnp.concatenate([found[:, q * batch : (q + 1) * batch] for q in range(4)], axis=0)[:vocab].astype(BF16)
     loads[1].wait()
-    partial = dot(counts, table[...])
+    partial = dot(counts, table[...], ((0,), (0,)))
     for i in range(8):
         for j in range(2):
-            text_out[:, j, i, :] = partial[j * n_sp : (j + 1) * n_sp, i * LANES : (i + 1) * LANES]
+            text_rows[:, 8 * j + i, :] = partial[j * n_sp : (j + 1) * n_sp, i * LANES : (i + 1) * LANES]
+    text_out[...] = text_rows[...].astype(BF16)
 
     loads[2].wait()
     coarse_f = coarse[...].astype(F32)
-    coarse_sums = jnp.concatenate(
+    coarse_box[sp] = jnp.concatenate(
         as_rows(jnp.sum(coarse_f, axis=0, keepdims=True))
         + as_rows(jnp.sum(coarse_f * coarse_f, axis=0, keepdims=True)),
         axis=0,
     )
-    for i in range(n_sp):
-        text_out[i, 2] = coarse_sums
 
     pl.semaphore_wait(barrier, jnp.where(owner, n_sp, n_sp + 1))
 
@@ -246,6 +249,7 @@
         remote(text_out.at[there], text_box.at[sp], send_sem.at[TEXT], recv_sem.at[TEXT], (dp, there)).start()
 
     text_box[sp] = text_out[sp]
+    to_spatial(coarse_box, COARSE)
 
     last = pixels - width
 
@@ -339,12 +343,12 @@
     turn_rows(width + own_pixels)
 
     receive(text_box, TEXT)
-    first_sums = total(text_box)
-    text_sum[...] = first_sums[0:2]
-    to_owners(lambda j: text_sum.at[j], text_dp_box, TEXT_DP)
+    text_sum[...] = jnp.sum(text_box[...].astype(F32), axis=0)
+    to_owners(lambda j: text_sum.at[pl.ds(8 * j, 8)], text_dp_box, TEXT_DP)
 
     later[1].wait()
-    coarse_total = group_total(first_sums[2], coarse.shape[1] // GROUPS)
+    receive(coarse_box, COARSE)
+    coarse_total = group_total(total(coarse_box), coarse.shape[1] // GROUPS)
     coarse_count = coarse.shape[0] * n_sp * (coarse.shape[1] // GROUPS)
     tiles = coarse.shape[1] // LANES
     c_mean = coarse_total[0:tiles, :] / coarse_count
@@ -380,7 +384,7 @@
 
     @pl.when(owner)
     def _():
-        text_dp_box[dp] = text_sum[dp % 2]
+        text_dp_box[dp] = text_sum[pl.ds(pl.multiple_of(8 * (dp % 2), 8), 8), :]
         receive(text_dp_box, TEXT_DP)
         pooled[...] = total(text_dp_box)
         from_owner(pooled, POOLED)
@@ -523,41 +527,47 @@
     back_box[sp] = sums_tile(first, second)
     to_spatial(back_box, BACK)
 
+    sides = []
     for side in range(2):
         wait_bytes(recv_sem.at[CUBE + side], cube_box.at[side, pl.ds(1, 7)])
         summed = cube_box[side, 0].astype(F32)
         for d in range(1, 8):
             summed = summed + cube_box[side, d].astype(F32)
-        weight_sum[side] = summed[0:half, :].T
+        sides.append(summed[0:half, :].T.reshape(16, part, half))
         tail_sum[side * 16 : (side + 1) * 16, :] = summed[half : half + 16, :]
+    weight_out[...] = jnp.concatenate(sides, axis=1).astype(BF16)
 
     def part_of(number):
-        rows = block_of((number // 4) % 4) * 32 + (number % 4) * part
-        return weight_sum.at[number // 16, pl.ds(pl.multiple_of(rows, part), part)]
-
-    @pl.loop(1, n_dp, unroll=True)
+        return weight_out.at[block_of(number // 4) * 4 + number % 4]
+
+    @pl.loop(0, 16, unroll=True)
     def _(i):
-        number = lax.rem(rank + i, n_dp)
-        remote(part_of(number), tile_box.at[rank], send_sem.at[TILE], recv_sem.at[TILE], of_rank(number)).start()
+        number = lax.rem(high_y * 4 + z_high + i, 16)
+
+        @pl.when(jnp.logical_or(i > 0, jnp.logical_not(gathers)))
+        def _():
+            remote(part_of(number), tile_box.at[rank], send_sem.at[TILE], recv_sem.at[TILE], gatherer(number)).start()
 
     for m in range(4):
-        number = quarter * 4 + m
-
-        @pl.when(number != rank)
+        itself = jnp.logical_and(owns_tail, z_high == m)
+
+        @pl.when(jnp.logical_not(itself))
         def _():
             remote(
                 tail_sum.at[pl.ds(m * part, part)],
                 tail_box.at[rank],
                 send_sem.at[TAIL],
                 recv_sem.at[TAIL],
-                of_rank(number),
+                gatherer(quarter * 4 + m),
             ).start()
 
-        @pl.when(number == rank)
+        @pl.when(itself)
         def _():
             tail_box[rank] = tail_sum[m * part : (m + 1) * part, :]
 
-    tile_box[rank] = part_of(rank)[...]
+    @pl.when(gathers)
+    def _():
+        tile_box[rank] = part_of(high_y * 4 + z_high)[...]
 
     receive(back_box, BACK)
     back = total(back_box)
@@ -603,7 +613,6 @@
         for i, (source, target) in enumerate(
             (
                 (out_ref, out_hbm), (grad_feat_ref, grad_feat_hbm),
-                (grad_mod_ref, grad_mod_hbm), (grad_conv_ref, grad_conv_hbm),
             )
         )
     ]
@@ -622,24 +631,41 @@
 
     stores[1].start()
 
-    receive(tile_box, TILE)
-    final_box[sp, 0] = total(tile_box)
-
-    def to_group(source):
+    final_slot = 2 * quarter + core
+
+    def to_group(rows):
         @pl.loop(1, n_sp, unroll=True)
         def _(i):
-            there = lax.rem(sp + i, n_sp)
-            remote(source, source, send_sem.at[FINAL], recv_sem.at[FINAL], (dp, there)).start()
+            remote(
+                final_own.at[rows],
+                final_hbm.at[final_slot, rows],
+                send_sem.at[FINAL],
+                recv_sem.at[FINAL],
+                (dp, lax.rem(sp + i, n_sp)),
+            ).start()
+
+    def own_final(rows):
+        return pltpu.make_async_copy(final_own.at[rows], final_hbm.at[final_slot, rows], store_sem.at[2])
+
+    main, both = pl.ds(0, 16), pl.ds(0, 32)
+    no_tail = jnp.logical_and(gathers, jnp.logical_not(owns_tail))
+
+    @pl.when(gathers)
+    def _():
+        receive(tile_box, TILE)
+        final_own[0:16, :] = jnp.sum(tile_box[...].astype(F32), axis=0).astype(BF16)
+
+    @pl.when(no_tail)
+    def _():
+        to_group(main)
+        own_final(main).start()
 
     @pl.when(owns_tail)
     def _():
         receive(tail_box, TAIL)
-        final_box[sp, 1] = total(tail_box)
-        to_group(final_box.at[sp])
-
-    @pl.when(jnp.logical_not(owns_tail))
-    def _():
-        to_group(final_box.at[sp, 0])
+        final_own[16:32, :] = jnp.concatenate([total(tail_box), jnp.zeros((part, half), F32)], axis=0).astype(BF16)
+        to_group(both)
+        own_final(both).start()
 
     @pl.when(quarter_owner)
     def _():
@@ -657,40 +683,51 @@
         mod_rows[...] = grads
         mod_start = pl.multiple_of((dp % in_lanes) * share, share)
         number = from_first // 4
-        grad_mod_parts[number] = mod_rows[pl.ds(mod_start, share), :].astype(BF16)
-        from_owner(grad_mod_parts.at[number], GRAD_MOD)
+        mod_own[...] = mod_rows[pl.ds(mod_start, share), :].astype(BF16)
+
+        @pl.loop(1, n_sp, unroll=True)
+        def _(i):
+            there = lax.rem(sp + i, n_sp)
+            remote(mod_own, mod_hbm.at[number], send_sem.at[GRAD_MOD], recv_sem.at[GRAD_MOD], (dp, there)).start()
+
+        pltpu.make_async_copy(mod_own, mod_hbm.at[number], store_sem.at[3]).start()
+
+    def units(count):
+        return tile_box.at[pl.ds(0, count)]
+
+    @pl.when(jnp.logical_not(gathers))
+    def _():
+        wait_bytes(recv_sem.at[FINAL], units(10))
+
+    @pl.when(no_tail)
+    def _():
+        wait_bytes(recv_sem.at[FINAL], units(9))
+        wait_bytes(send_sem.at[FINAL], units(n_sp - 1))
+        wait_bytes(send_sem.at[TILE], units(15))
+        own_final(main).wait()
 
     @pl.when(owns_tail)
     def _():
-        wait_bytes(recv_sem.at[FINAL], tile_box.at[pl.ds(0, n_sp)])
-
-    @pl.when(jnp.logical_not(owns_tail))
-    def _():
-        wait_bytes(recv_sem.at[FINAL], tile_box.at[pl.ds(0, n_sp + 1)])
-
-    holders = [
-        8 * (tap // 4) + 2 * (2 * (tap % 2) + (tap // 2) % 2) + side for tap in range(8) for side in range(2)
-    ]
-    tail_place = (high_y // 2) * 8 + (high_y % 2) * 2
-    grad_conv_ref[...] = jnp.concatenate(
-        [final_box[j, 0] for j in holders] + [final_box[tail_place, 1], final_box[tail_place + 1, 1]], axis=1
-    ).astype(BF16)
-
-    stores[3].start()
+        wait_bytes(recv_sem.at[FINAL], units(8))
+        wait_bytes(send_sem.at[FINAL], units(2 * (n_sp - 1)))
+        wait_bytes(send_sem.at[TILE], units(15))
+        own_final(both).wait()
+
+    @pl.when(jnp.logical_not(gathers))
+    def _():
+        wait_bytes(send_sem.at[TILE], units(16))
 
     @pl.when(quarter_owner)
     def _():
-        wait_bytes(recv_sem.at[GRAD_MOD], grad_mod_parts.at[pl.ds(0, 3)])
+        wait_bytes(recv_sem.at[GRAD_MOD], mod_hbm.at[pl.ds(0, 3)])
+        pltpu.make_async_copy(mod_own, mod_hbm.at[from_first // 4], store_sem.at[3]).wait()
 
     @pl.when(jnp.logical_not(quarter_owner))
     def _():
-        wait_bytes(recv_sem.at[GRAD_MOD], grad_mod_parts)
-
-    grad_mod_ref[...] = jnp.concatenate([grad_mod_parts[i] for i in range(4)], axis=1)
-    stores[2].start()
+        wait_bytes(recv_sem.at[GRAD_MOD], mod_hbm)
 
     for box, index in (
-        (fine_box, FINE), (back_box, BACK), (text_box, TEXT), (tile_box, TILE),
+        (fine_box, FINE), (back_box, BACK), (text_box, TEXT), (coarse_box, COARSE),
     ):
         wait_bytes(send_sem.at[index], others(box))
 
@@ -701,8 +738,7 @@
     @pl.when(quarter_owner)
     def _():
         wait_bytes(send_sem.at[MOD], mod_box.at[pl.ds(0, 7)])
-        rows = (n_sp - 1) * grad_mod_parts.shape[1] // 2
-        wait_bytes(send_sem.at[GRAD_MOD], hidden.at[pl.ds(0, rows)])
+        wait_bytes(send_sem.at[GRAD_MOD], units(2 * (n_sp - 1)))
 
     @pl.when(jnp.logical_not(quarter_owner))
     def _():
@@ -725,25 +761,28 @@
     @pl.when(owns_tail)
     def _():
         wait_bytes(send_sem.at[TAIL], tail_box.at[pl.ds(0, 3)])
-        wait_bytes(send_sem.at[FINAL], tile_box.at[pl.ds(0, 2 * (n_sp - 1))])
 
     @pl.when(jnp.logical_not(owns_tail))
     def _():
         wait_bytes(send_sem.at[TAIL], tail_box.at[pl.ds(0, 4)])
-        wait_bytes(send_sem.at[FINAL], tile_box.at[pl.ds(0, n_sp - 1)])
 
     for store in stores:
         store.wait()
 
 
-def write(*refs):
-    sources, targets, rooms, load_sem, store_sem = refs[:4], refs[4:8], refs[8:12], refs[12], refs[13]
+def write(
+    out, grad_feat, final, mod, out_hbm, grad_feat_hbm, grad_conv_hbm, grad_mod_hbm,
+    out_room, grad_feat_room, final_room, mod_room, grad_conv, grad_mod, load_sem, store_sem,
+):
+    fetch_final = pltpu.make_async_copy(final, final_room, load_sem.at[4])
+    fetch_mod = pltpu.make_async_copy(mod, mod_room, load_sem.at[5])
+    fetch_final.start()
+    fetch_mod.start()
     moves = []
-    for source, room, target in zip(sources, rooms, targets):
-        rows = source.shape[0]
-        pieces = 4 if rows >= 1024 else 1
-        for i in range(pieces):
-            piece = pl.ds(i * rows // pieces, rows // pieces)
+    for source, room, target in ((out, out_room, out_hbm), (grad_feat, grad_feat_room, grad_feat_hbm)):
+        rows = source.shape[0] // 2
+        for i in range(2):
+            piece = pl.ds(i * rows, rows)
             number = len(moves)
             moves.append(
                 (
@@ -753,10 +792,27 @@
             )
     for fetch, _ in moves:
         fetch.start()
+    fetch_final.wait()
+    parts = final_room[...].astype(F32)
+    tail_quarter = lax.axis_index("dp") // 8
+    columns = [
+        parts[2 * (tap // 2) + side, 8 * (tap % 2) : 8 * (tap % 2) + 8, :] for tap in range(8) for side in range(2)
+    ] + [final_room[2 * tail_quarter + side].astype(F32)[16:24, :] for side in range(2)]
+    grad_conv[...] = jnp.concatenate(columns, axis=1).astype(BF16)
+    fetch_mod.wait()
+    grad_mod[...] = jnp.concatenate([mod_room[i] for i in range(4)], axis=1)
+    last = [
+        pltpu.make_async_copy(grad_conv, grad_conv_hbm, store_sem.at[4]),
+        pltpu.make_async_copy(grad_mod, grad_mod_hbm, store_sem.at[5]),
+    ]
+    for store in last:
+        store.start()
     for fetch, store in moves:
         fetch.wait()
         store.start()
     for _, store in moves:
+        store.wait()
+    for store in last:
         store.wait()
 
 
@@ -774,8 +830,6 @@
     scratch = [
         vm((pixels, channels), BF16),
         vm((pixels, channels), BF16),
-        vm((part, taps * channels), BF16),
-        vm((mod_rows, 2 * channels), BF16),
         vm(text_ids.shape, jnp.int32),
         vm((pixels, channels), BF16),
         vm((cells, coarse_width), BF16),
@@ -801,33 +855,39 @@
         vm((pixels, channels), F32),
         vm((n_sp,) + tile, F32),
         vm((n_sp,) + tile, F32),
-        vm((n_sp, 3) + tile, F32),
-        vm((n_sp, 3) + tile, F32),
-        vm((2,) + tile, F32),
+        vm((n_sp,) + tile, F32),
+        vm((n_sp, 16, LANES), F32),
+        vm((n_sp, 16, LANES), BF16),
+        vm((n_sp, 16, LANES), BF16),
+        vm((16, LANES), F32),
         vm((n_dp,) + tile, F32),
         vm(tile, F32),
         vm((4,) + tile, F32),
         vm((n_dp,) + tile, F32),
         vm((LANES, LANES), F32),
-        vm((4, mod_rows, LANES), BF16),
+        vm((mod_rows, LANES), BF16),
         vm((3, 3 * half, channels), F32),
         vm((2, 4, 2, half + 16, half), BF16),
         vm((2, 8, half + 16, half), BF16),
-        vm((2, half, half), F32),
+        vm((16, 2 * part, half), BF16),
         vm((32, half), F32),
+        vm((n_dp, 2 * part, half), BF16),
         vm((n_dp, part, half), F32),
-        vm((n_dp, part, half), F32),
-        vm((n_sp, 2, part, half), F32),
+        vm((32, half), BF16),
         pltpu.SemaphoreType.DMA((8,)),
         pltpu.SemaphoreType.DMA((4,)),
         pltpu.SemaphoreType.DMA((4,)),
         pltpu.SemaphoreType.DMA((4,)),
-        pltpu.SemaphoreType.DMA((15,)),
-        pltpu.SemaphoreType.DMA((15,)),
+        pltpu.SemaphoreType.DMA((16,)),
+        pltpu.SemaphoreType.DMA((16,)),
     ]
     shapes = (
         jax.ShapeDtypeStruct((pixels, channels), BF16),
         jax.ShapeDtypeStruct((pixels, channels), BF16),
+        jax.ShapeDtypeStruct((8, 32, half), BF16),
+        jax.ShapeDtypeStruct((4, mod_rows, LANES), BF16),
+    )
+    written = shapes[:2] + (
         jax.ShapeDtypeStruct((part, taps * channels), BF16),
         jax.ShapeDtypeStruct((mod_rows, 2 * channels), BF16),
     )
@@ -853,11 +913,11 @@
     )
     output, grad_features, grad_conv, grad_mod = pl.pallas_call(
         write,
-        out_shape=shapes,
+        out_shape=written,
         in_specs=[anywhere] * 4,
         out_specs=(anywhere,) * 4,
-        scratch_shapes=[vm(shape.shape, shape.dtype) for shape in shapes]
-        + [pltpu.SemaphoreType.DMA((10,)), pltpu.SemaphoreType.DMA((10,))],
+        scratch_shapes=[vm(shape.shape, shape.dtype) for shape in shapes + written[2:]]
+        + [pltpu.SemaphoreType.DMA((6,)), pltpu.SemaphoreType.DMA((6,))],
         compiler_params=pltpu.CompilerParams(vmem_limit_bytes=VMEM_LIMIT),
     )(*results)
     return output.reshape(features.shape), grad_features.reshape(features.shape), grad_conv, grad_mod

time: 59.8 us -> 56.9 us (0.952)
  Pallas kernels: 58.3 us -> 55.4 us
    pallas_call x1, Pallas kernels: 56.2 us -> 53.3 us  [body(): pl.pallas_call(functools.partial(kernel, n_dp, n_sp, tile_rows, width), o...]
where the time goes in v3:
time: 56.9 us; the launch traced here: 56.7 us
  Pallas kernels  55.4 us (97%)
  between operations  1.29 us (2%)
    pallas_call x1, Pallas kernels, body(): pl.pallas_call(functools.partial(kernel, n_dp, n_sp, tile_rows, width), o...  53.3 us
    pallas_call x1, Pallas kernels, body(): pl.pallas_call(write, out_shape=written, in_specs=[anywhere] * 4, out_spe...  2.08 us

profile of v3, /device:TPU:1, one launch (start us, length us, event | category | flops | bytes accessed | tf_op | source)
XLA Modules:
  0.0 56.7 jit_solution(13699004999664359953)
XLA Ops:
  1.3 53.3 %shard_map.120 = (bf16[1024,256]{1,0:T(8,128)(2,1)}, bf16[1024,256]{1,0:T(8,128)(2,1)}, bf16[8,32,128]{2,1,0:T(8,128)(2,1)}, bf16[4,32,128]{2,1,0:T(8,128)(2,1)}) custom-call(s32[1]{0:T(128)S(6)} %copy.13.refs_0_, s32[32,128]{1,0:T(8,128)} %refs_1_.1, bf16[1024,256]{1,0:T(8,128)(2,1)} %bitcast.5, bf16[64,512]{1,0:T(8,128)(2,1)} %bitcast.7, ...), custom_call_target="tpu_custom_call" | custom-call | tf_op jit(solution)/shard_map/pallas_call | solution.py:894
  54.6 2.1 %shard_map.121 = (bf16[1024,256]{1,0:T(8,128)(2,1)}, bf16[1024,256]{1,0:T(8,128)(2,1)}, bf16[8,2304]{1,0:T(8,128)(2,1)}, bf16[32,512]{1,0:T(8,128)(2,1)}) custom-call(bf16[1024,256]{1,0:T(8,128)(2,1)} %get-tuple-element.12.out, bf16[1024,256]{1,0:T(8,128)(2,1)} %get-tuple-element.13.grad_feat, bf16[8,32,128]{2,1,0:T(8,128)(2,1)} %get-tuple-element.14.final, ...), custom_call_target="tpu_custom_call" | custom-call | tf_op jit(solution)/shard_map/pallas_call | solution.py:914

commit v4 on v3

--- a/solution.py
+++ b/solution.py
@@ -78,7 +78,7 @@
         feat, coarse, table, w_mod, w_skip, w_conv, w_stack, cot,
         cot_edge, far_edge, hid_edge, cot_half, cot_chip, cot_spread, cot_turned, hid_spread, chosen, up, merged,
         hidden, hidden_pair, grad_hid,
-        coarse_box, fine_box, back_box, text_rows, text_out, text_box, text_sum, text_dp_box, pooled,
+        coarse_box, fine_box, back_box, text_rows, text_out, text_box, text_sum, text_dp_box, pooled, time_part,
         mod_out, mod_box, mod_rows, mod_own, weight_own, cube_out, cube_box, weight_out, tail_sum,
         tile_box, tail_box, final_own,
         load_sem, store_sem, edge_send, edge_recv, send_sem, recv_sem,
@@ -144,7 +144,7 @@
         load(w_mod_hbm, w_mod, 6),
         load(w_conv_hbm, w_conv, 7),
     ]
-    for copy in loads:
+    for copy in loads[:2]:
         copy.start()
 
     barrier = pltpu.get_barrier_semaphore()
@@ -162,7 +162,7 @@
         def _(i):
             greet((lax.rem(dp + i, n_dp), sp))
 
-    for copy in later:
+    for copy in loads[2:] + later:
         copy.start()
 
     def remote(source, target, send, recv, place):
@@ -326,6 +326,12 @@
     def _():
         far.start()
 
+    row, lane = iota((8, LANES), 0), iota((8, LANES), 1)
+    half_width = 4 * LANES
+    index = ((row & 3) * LANES + lane).astype(F32)
+    angle = time_ref[0].astype(F32) * jnp.exp(-math.log(10000.0) * index / half_width)
+    time_part[...] = jnp.where(row < 4, jnp.sin(angle), jnp.cos(angle))
+
     shape = chosen.shape
     coarse_cols = width // 4
     place = iota(shape, 0)
@@ -406,15 +412,18 @@
     turned_shifts(jnp.where(core == 0, near, farther), cot_turned, 0)
     turned_shifts(jnp.where(core == 0, farther, near), cot_turned, width + 2 * pixels)
 
+    receive(fine_box, FINE)
+    fine_total = group_total(total(fine_box), channels // GROUPS)
+    fine_count = pixels * n_sp * (channels // GROUPS)
+    f_mean = fine_total[0:2, :] / fine_count
+    f_scale = lax.rsqrt(fine_total[2:4, :] / fine_count - f_mean * f_mean + EPS)
+    center, scale = as_row(f_mean, 0, 2), as_row(f_scale, 0, 2)
+
     @pl.when(jnp.logical_not(owner))
     def _():
         wait_bytes(recv_sem.at[POOLED], pooled)
 
-    row, lane = iota((8, LANES), 0), iota((8, LANES), 1)
-    half_width = 4 * LANES
-    index = ((row & 3) * LANES + lane).astype(F32)
-    angle = time_ref[0].astype(F32) * jnp.exp(-math.log(10000.0) * index / half_width)
-    embed = jnp.where(row < 4, jnp.sin(angle), jnp.cos(angle)) + pooled[...] / tokens
+    embed = time_part[...] + pooled[...] / tokens
     embed = (embed * sigmoid(embed)).astype(BF16).astype(F32)
     later[2].wait()
     embed_row = jnp.broadcast_to(as_row(embed, 0, 8), (8, 8 * LANES)).astype(BF16)
@@ -422,17 +431,13 @@
     gain = 1.0 + modulation[:, :channels]
     shift = modulation[:, channels:]
 
-    receive(fine_box, FINE)
-    fine_total = group_total(total(fine_box), channels // GROUPS)
-    fine_count = pixels * n_sp * (channels // GROUPS)
-    f_mean = fine_total[0:2, :] / fine_count
-    f_scale = lax.rsqrt(fine_total[2:4, :] / fine_count - f_mean * f_mean + EPS)
-    center, scale = as_row(f_mean, 0, 2), as_row(f_scale, 0, 2)
+    factor = scale * gain
+    term_of_hidden = shift - center * factor
 
     @pl.loop(0, tile_rows, unroll=True)
     def _(r):
         start = pl.multiple_of(r * width, width)
-        pre = (merged[pl.ds(start, width), :].astype(F32) - center) * scale * gain + shift
+        pre = merged[pl.ds(start, width), :].astype(F32) * factor + term_of_hidden
         act = pre * sigmoid(pre)
         hidden[pl.ds(start, width), :] = act.astype(BF16)
         low, high = act[:, :half], act[:, half:]
@@ -456,9 +461,27 @@
     for dr in range(3):
         weight_own[dr] = weight_term(dr, own_pixels)
     wait_bytes(recv_sem.at[PAIR_HIDDEN], hidden_pair.at[pl.ds(0, pixels)])
-    for dr in range(3):
+    def send_shares(their_quarter):
+        dx = odd_x + their_quarter % 2 - 2 * odd_x * (their_quarter % 2)
+        dz = odd_z + their_quarter // 2 - 2 * odd_z * (their_quarter // 2)
+        for dy in range(2):
+            their_y = odd_y + dy - 2 * odd_y * dy
+            d = dx + 2 * dy + 4 * dz
+
+            @pl.when(d > 0)
+            def _():
+                for side in range(2):
+                    remote(
+                        cube_out.at[side, their_quarter, their_y],
+                        cube_box.at[side, d],
+                        send_sem.at[CUBE + side],
+                        recv_sem.at[CUBE + side],
+                        neighbour(side, d),
+                    ).start()
+
+    for dr in (2, 1, 0):
         grads = weight_own[dr] + weight_term(dr, other_pixels)
-        for dc in range(3):
+        for dc in (2, 1, 0):
             tap = 3 * dr + dc
             grad = grads[dc * half : (dc + 1) * half, :]
             if tap < 8:
@@ -470,19 +493,9 @@
                     for number in range(8):
                         first = (number % 2) * half + block_of(number // 2) * 32 + side * 16
                         cube_out[side, number // 2, number % 2, half : half + 16] = turned[first : first + 16, :]
-
-    for side in range(2):
-        for d in range(1, 8):
-            dx, dy, dz = d % 2, (d // 2) % 2, d // 4
-            their_quarter = 2 * (odd_z + dz - 2 * odd_z * dz) + (odd_x + dx - 2 * odd_x * dx)
-            their_y = odd_y + dy - 2 * odd_y * dy
-            remote(
-                cube_out.at[side, their_quarter, their_y],
-                cube_box.at[side, d],
-                send_sem.at[CUBE + side],
-                recv_sem.at[CUBE + side],
-                neighbour(side, d),
-            ).start()
+        for their_quarter in ((0, 1), (2,), (3,))[dr]:
+            send_shares(their_quarter)
+
     for side in range(2):
         cube_box[side, 0] = cube_out[side, quarter, odd_y]
 
@@ -622,15 +635,6 @@
     means = group_total(back[0:4, :] * gain_tile, channels // GROUPS) / fine_count
     mean_two, mean_one = as_row(means, 0, 2), as_row(means, 2, 2)
 
-    @pl.loop(0, tile_rows, unroll=True)
-    def _(r):
-        start = pl.multiple_of(r * width, width)
-        normed = (merged[pl.ds(start, width), :].astype(F32) - center) * scale
-        inner = grad_hid[pl.ds(start, width), :] * gain - mean_one - normed * mean_two
-        grad_feat_ref[pl.ds(start, width), :] = (cot[pl.ds(start, width), :].astype(F32) + scale * inner).astype(BF16)
-
-    stores[1].start()
-
     final_slot = 2 * quarter + core
 
     def to_group(rows):
@@ -666,6 +670,15 @@
         final_own[16:32, :] = jnp.concatenate([total(tail_box), jnp.zeros((part, half), F32)], axis=0).astype(BF16)
         to_group(both)
         own_final(both).start()
+
+    @pl.loop(0, tile_rows, unroll=True)
+    def _(r):
+        start = pl.multiple_of(r * width, width)
+        normed = (merged[pl.ds(start, width), :].astype(F32) - center) * scale
+        inner = grad_hid[pl.ds(start, width), :] * gain - mean_one - normed * mean_two
+        grad_feat_ref[pl.ds(start, width), :] = (cot[pl.ds(start, width), :].astype(F32) + scale * inner).astype(BF16)
+
+    stores[1].start()
 
     @pl.when(quarter_owner)
     def _():
@@ -861,6 +874,7 @@
         vm((n_sp, 16, LANES), BF16),
         vm((16, LANES), F32),
         vm((n_dp,) + tile, F32),
+        vm(tile, F32),
         vm(tile, F32),
         vm((4,) + tile, F32),
         vm((n_dp,) + tile, F32),

time: 56.9 us -> 55.3 us (0.972)
  Pallas kernels: 55.4 us -> 53.9 us
    pallas_call x1, Pallas kernels: 53.3 us -> 51.8 us  [body(): pl.pallas_call(functools.partial(kernel, n_dp, n_sp, tile_rows, width), o...]
where the time goes in v4:
time: 55.3 us; the launch traced here: 55.1 us
  Pallas kernels  53.9 us (97%)
  between operations  1.29 us (2%)
    pallas_call x1, Pallas kernels, body(): pl.pallas_call(functools.partial(kernel, n_dp, n_sp, tile_rows, width), o...  51.8 us
    pallas_call x1, Pallas kernels, body(): pl.pallas_call(write, out_shape=written, in_specs=[anywhere] * 4, out_spe...  2.08 us

profile of v4, /device:TPU:1, one launch (start us, length us, event | category | flops | bytes accessed | tf_op | source)
XLA Modules:
  0.0 55.1 jit_solution(11940196026926467203)
XLA Ops:
  1.3 51.8 %shard_map.120 = (bf16[1024,256]{1,0:T(8,128)(2,1)}, bf16[1024,256]{1,0:T(8,128)(2,1)}, bf16[8,32,128]{2,1,0:T(8,128)(2,1)}, bf16[4,32,128]{2,1,0:T(8,128)(2,1)}) custom-call(s32[1]{0:T(128)S(6)} %copy.13.refs_0_, s32[32,128]{1,0:T(8,128)} %refs_1_.1, bf16[1024,256]{1,0:T(8,128)(2,1)} %bitcast.5, bf16[64,512]{1,0:T(8,128)(2,1)} %bitcast.7, ...), custom_call_target="tpu_custom_call" | custom-call | tf_op jit(solution)/shard_map/pallas_call | solution.py:908
  53.1 2.1 %shard_map.121 = (bf16[1024,256]{1,0:T(8,128)(2,1)}, bf16[1024,256]{1,0:T(8,128)(2,1)}, bf16[8,2304]{1,0:T(8,128)(2,1)}, bf16[32,512]{1,0:T(8,128)(2,1)}) custom-call(bf16[1024,256]{1,0:T(8,128)(2,1)} %get-tuple-element.12.out, bf16[1024,256]{1,0:T(8,128)(2,1)} %get-tuple-element.13.grad_feat, bf16[8,32,128]{2,1,0:T(8,128)(2,1)} %get-tuple-element.14.final, ...), custom_call_target="tpu_custom_call" | custom-call | tf_op jit(solution)/shard_map/pallas_call | solution.py:928

commit v5 on v4

--- a/solution.py
+++ b/solution.py
@@ -152,15 +152,15 @@
     def greet(place):
         pl.semaphore_signal(barrier, inc=1, device_id=place, device_id_type=MESH)
 
+    @pl.when(owner)
+    def _():
+        @pl.loop(1, n_dp)
+        def _(i):
+            greet((lax.rem(dp + i, n_dp), sp))
+
     @pl.loop(1, n_sp, unroll=True)
     def _(i):
         greet((dp, lax.rem(sp + i, n_sp)))
-
-    @pl.when(owner)
-    def _():
-        @pl.loop(1, n_dp)
-        def _(i):
-            greet((lax.rem(dp + i, n_dp), sp))
 
     for copy in loads[2:] + later:
         copy.start()
@@ -346,8 +346,6 @@
             start = pl.multiple_of(first_row + r * width, width)
             turned_shifts(cot_chip[pl.ds(start, width), :].astype(F32), cot_turned, start)
 
-    turn_rows(width + own_pixels)
-
     receive(text_box, TEXT)
     text_sum[...] = jnp.sum(text_box[...].astype(F32), axis=0)
     to_owners(lambda j: text_sum.at[pl.ds(8 * j, 8)], text_dp_box, TEXT_DP)
@@ -395,6 +393,7 @@
         pooled[...] = total(text_dp_box)
         from_owner(pooled, POOLED)
 
+    turn_rows(width + own_pixels)
     wait_bytes(recv_sem.at[PAIR_COT], cot_chip.at[own_rows])
     turn_rows(width + other_pixels)
     receive_edges(cot, cot_edge, 0)

time: 55.3 us -> 55.5 us (level)
  no operation moved by 1% of the time
where the time goes in v5:
time: 55.5 us; the launch traced here: 55.3 us
  Pallas kernels  54 us (97%)
  between operations  1.29 us (2%)
    pallas_call x1, Pallas kernels, body(): pl.pallas_call(functools.partial(kernel, n_dp, n_sp, tile_rows, width), o...  51.9 us
    pallas_call x1, Pallas kernels, body(): pl.pallas_call(write, out_shape=written, in_specs=[anywhere] * 4, out_spe...  2.08 us

profile of v5, /device:TPU:1, one launch (start us, length us, event | category | flops | bytes accessed | tf_op | source)
XLA Modules:
  0.0 55.3 jit_solution(2456682312653624331)
XLA Ops:
  1.3 51.9 %shard_map.120 = (bf16[1024,256]{1,0:T(8,128)(2,1)}, bf16[1024,256]{1,0:T(8,128)(2,1)}, bf16[8,32,128]{2,1,0:T(8,128)(2,1)}, bf16[4,32,128]{2,1,0:T(8,128)(2,1)}) custom-call(s32[1]{0:T(128)S(6)} %copy.13.refs_0_, s32[32,128]{1,0:T(8,128)} %refs_1_.1, bf16[1024,256]{1,0:T(8,128)(2,1)} %bitcast.5, bf16[64,512]{1,0:T(8,128)(2,1)} %bitcast.7, ...), custom_call_target="tpu_custom_call" | custom-call | tf_op jit(solution)/shard_map/pallas_call | solution.py:907
  53.2 2.1 %shard_map.121 = (bf16[1024,256]{1,0:T(8,128)(2,1)}, bf16[1024,256]{1,0:T(8,128)(2,1)}, bf16[8,2304]{1,0:T(8,128)(2,1)}, bf16[32,512]{1,0:T(8,128)(2,1)}) custom-call(bf16[1024,256]{1,0:T(8,128)(2,1)} %get-tuple-element.12.out, bf16[1024,256]{1,0:T(8,128)(2,1)} %get-tuple-element.13.grad_feat, bf16[8,32,128]{2,1,0:T(8,128)(2,1)} %get-tuple-element.14.final, ...), custom_call_target="tpu_custom_call" | custom-call | tf_op jit(solution)/shard_map/pallas_call | solution.py:927

commit v6 on v5

--- a/solution.py
+++ b/solution.py
@@ -49,15 +49,14 @@
     return [row[:, i * LANES : (i + 1) * LANES] for i in range(row.shape[1] // LANES)]
 
 
-def column_shifts(rows, spread_ref, first_row, reverse):
-    width, channels = rows.shape
-    column = iota(rows.shape, 0)
-    earlier = jnp.where(column == 0, 0.0, pltpu.roll(rows, 1, 0)).astype(BF16)
-    later = jnp.where(column == width - 1, 0.0, pltpu.roll(rows, width - 1, 0)).astype(BF16)
-    left, right = (later, earlier) if reverse else (earlier, later)
-    spread_ref[pl.ds(first_row, width), 0:channels] = left
-    spread_ref[pl.ds(first_row, width), channels : 2 * channels] = rows.astype(BF16)
-    spread_ref[pl.ds(first_row, width), 2 * channels : 3 * channels] = right
+def from_neighbours(earlier, here, later, width):
+    rows = here.shape[0]
+    column = iota(here.shape, 0) & (width - 1)
+    return (
+        here
+        + jnp.where(column == 0, 0.0, pltpu.roll(earlier, 1, 0))
+        + jnp.where(column == width - 1, 0.0, pltpu.roll(later, rows - 1, 0))
+    )
 
 
 def turned_shifts(rows, turned_ref, first_pixel):
@@ -75,9 +74,8 @@
         time_ref, ids_hbm, feat_hbm, coarse_hbm, table_hbm, w_mod_hbm, w_skip_hbm, w_conv_hbm, cot_hbm,
         out_hbm, grad_feat_hbm, final_hbm, mod_hbm,
         out_ref, grad_feat_ref, ids_ref,
-        feat, coarse, table, w_mod, w_skip, w_conv, w_stack, cot,
-        cot_edge, far_edge, hid_edge, cot_half, cot_chip, cot_spread, cot_turned, hid_spread, chosen, up, merged,
-        hidden, hidden_pair, grad_hid,
+        feat, coarse, table, w_mod, w_skip, w_conv, cot_rows,
+        far_edge, cot_half, cot_chip, cot_turned, chosen, up, merged, hid_rows, hidden_pair, grad_hid,
         coarse_box, fine_box, back_box, text_rows, text_out, text_box, text_sum, text_dp_box, pooled, time_part,
         mod_out, mod_box, mod_rows, mod_own, weight_own, cube_out, cube_box, weight_out, tail_sum,
         tile_box, tail_box, final_own,
@@ -87,6 +85,7 @@
     pixels = tile_rows * width
     half = channels // 2
     part = channels // n_dp
+    cot, hidden = (ref.at[pl.ds(width, pixels)] for ref in (cot_rows, hid_rows))
     dp = lax.axis_index("dp")
     sp = lax.axis_index("spatial")
     chip, core = sp // 2, sp % 2
@@ -115,6 +114,19 @@
         return ((2 * y_there + odd_y) * 4 + z_there, z_low * 8 + (2 * (z_there % 2) + odd_x) * 2 + core)
 
     gathers = high_x == z_high % 2
+    group = []
+    for dz, dx, dc in (
+        (1, 2, 0), (1, 2, 1), (1, 1, 0), (1, 1, 1), (1, 3, 0), (1, 3, 1), (0, 2, 0), (0, 2, 1),
+        (1, 0, 0), (1, 0, 1), (0, 1, 0), (0, 1, 1), (0, 3, 0), (0, 3, 1), (0, 0, 1),
+    ):
+        group.append(lax.rem(z_low + dz, 2) * 8 + lax.rem(x + dx, 4) * 2 + lax.rem(core + dc, 2))
+    high_steps = sorted(
+        ((dy, dz) for dy in range(4) for dz in range(4)), key=lambda s: -min(s[0], 4 - s[0]) - min(s[1], 4 - s[1])
+    )
+    dp_steps = sorted(
+        ((dy, dz) for dy in range(8) for dz in range(4)), key=lambda s: -min(s[0], 8 - s[0]) - 2 * min(s[1], 4 - s[1])
+    )[:-1]
+
     owns_tail = jnp.logical_and(gathers, high_y == quarter)
     owner = dp // 2 == sp
     from_first = lax.rem(sp - dp // 2 + n_sp, n_sp)
@@ -154,13 +166,11 @@
 
     @pl.when(owner)
     def _():
-        @pl.loop(1, n_dp)
-        def _(i):
-            greet((lax.rem(dp + i, n_dp), sp))
-
-    @pl.loop(1, n_sp, unroll=True)
-    def _(i):
-        greet((dp, lax.rem(sp + i, n_sp)))
+        for dy, dz in dp_steps:
+            greet((lax.rem(y + dy, 8) * 4 + lax.rem(z_high + dz, 4), sp))
+
+    for there in group:
+        greet((dp, there))
 
     for copy in loads[2:] + later:
         copy.start()
@@ -174,9 +184,7 @@
         pltpu.make_async_copy(ref, ref, sem).wait()
 
     def to_spatial(box, index):
-        @pl.loop(1, n_sp, unroll=True)
-        def _(i):
-            there = lax.rem(sp + i, n_sp)
+        for there in group:
             remote(box.at[sp], box.at[sp], send_sem.at[index], recv_sem.at[index], (dp, there)).start()
 
     def to_owners(source_of, box, index):
@@ -197,9 +205,7 @@
             wait_bytes(send_sem.at[index], box.at[pl.ds(0, 2)])
 
     def from_owner(ref, index):
-        @pl.loop(1, n_sp, unroll=True)
-        def _(i):
-            there = lax.rem(sp + i, n_sp)
+        for there in group:
             remote(ref, ref, send_sem.at[index], recv_sem.at[index], (dp, there)).start()
 
     def others(box):
@@ -243,27 +249,33 @@
 
     pl.semaphore_wait(barrier, jnp.where(owner, n_sp, n_sp + 1))
 
-    @pl.loop(1, n_sp, unroll=True)
-    def _(i):
-        there = lax.rem(sp + i, n_sp)
+    to_spatial(coarse_box, COARSE)
+    for there in group:
         remote(text_out.at[there], text_box.at[sp], send_sem.at[TEXT], recv_sem.at[TEXT], (dp, there)).start()
 
     text_box[sp] = text_out[sp]
-    to_spatial(coarse_box, COARSE)
 
     last = pixels - width
 
-    def edges(source, target, first):
+    def edges(rows, first):
         down = remote(
-            source.at[pl.ds(last, width)], target.at[0], edge_send.at[first], edge_recv.at[first], (dp, sp + 1)
+            rows.at[pl.ds(pixels, width)],
+            rows.at[pl.ds(0, width)],
+            edge_send.at[first],
+            edge_recv.at[first],
+            (dp, sp + 1),
         )
         upward = remote(
-            source.at[pl.ds(0, width)], target.at[1], edge_send.at[first + 1], edge_recv.at[first + 1], (dp, sp - 1)
+            rows.at[pl.ds(width, width)],
+            rows.at[pl.ds(width + pixels, width)],
+            edge_send.at[first + 1],
+            edge_recv.at[first + 1],
+            (dp, sp - 1),
         )
         return down, upward
 
-    def start_edges(source, target, first):
-        down, upward = edges(source, target, first)
+    def start_edges(rows, first):
+        down, upward = edges(rows, first)
 
         @pl.when(sp < n_sp - 1)
         def _():
@@ -273,8 +285,8 @@
         def _():
             upward.start()
 
-    def receive_edges(source, target, first):
-        down, upward = edges(source, target, first)
+    def receive_edges(rows, first):
+        down, upward = edges(rows, first)
 
         @pl.when(sp > 0)
         def _():
@@ -286,14 +298,14 @@
 
         @pl.when(sp == 0)
         def _():
-            target[0] = jnp.zeros((width, channels), BF16)
+            rows[0:width, :] = jnp.zeros((width, channels), BF16)
 
         @pl.when(sp == n_sp - 1)
         def _():
-            target[1] = jnp.zeros((width, channels), BF16)
-
-    def finish_edges(source, target, first):
-        down, upward = edges(source, target, first)
+            rows[width + pixels :, :] = jnp.zeros((width, channels), BF16)
+
+    def finish_edges(rows, first):
+        down, upward = edges(rows, first)
 
         @pl.when(sp < n_sp - 1)
         def _():
@@ -304,7 +316,7 @@
             upward.wait_send()
 
     loads[3].wait()
-    start_edges(cot, cot_edge, 0)
+    start_edges(cot_rows, 0)
     cot_half[...] = cot[:, other_lanes]
     cot_chip[own_rows, :] = cot[:, own_lanes]
     pair_cot = remote(
@@ -396,7 +408,7 @@
     turn_rows(width + own_pixels)
     wait_bytes(recv_sem.at[PAIR_COT], cot_chip.at[own_rows])
     turn_rows(width + other_pixels)
-    receive_edges(cot, cot_edge, 0)
+    receive_edges(cot_rows, 0)
 
     @pl.when(takes_far)
     def _():
@@ -406,7 +418,7 @@
     def _():
         far_edge[...] = jnp.zeros((width, half), BF16)
 
-    near = cot_edge[core, :, own_lanes].astype(F32)
+    near = cot_rows[pl.ds(pl.multiple_of(core * (width + pixels), width), width), own_lanes].astype(F32)
     farther = far_edge[...].astype(F32)
     turned_shifts(jnp.where(core == 0, near, farther), cot_turned, 0)
     turned_shifts(jnp.where(core == 0, farther, near), cot_turned, width + 2 * pixels)
@@ -498,30 +510,27 @@
     for side in range(2):
         cube_box[side, 0] = cube_out[side, quarter, odd_y]
 
-    start_edges(hidden, hid_edge, 2)
-
-    @pl.loop(0, tile_rows, unroll=True)
-    def _(r):
-        start = pl.multiple_of(r * width, width)
-        column_shifts(cot[pl.ds(start, width), :].astype(F32), cot_spread, pl.multiple_of(start + width, width), True)
-
-    column_shifts(cot_edge[0].astype(F32), cot_spread, 0, True)
-    column_shifts(cot_edge[1].astype(F32), cot_spread, pixels + width, True)
+    start_edges(hid_rows, 2)
+
     later[3].wait()
     chunk = pixels // 2
 
     @pl.loop(0, 2)
     def _(c):
         start = pl.multiple_of(c * chunk, chunk)
-        grad = None
-        for dr in range(3):
-            term = dot(
-                cot_spread[pl.ds(pl.multiple_of(start + (2 - dr) * width, width), chunk), :],
-                w_conv[:, 3 * dr * channels : 3 * (dr + 1) * channels],
-                ((1,), (1,)),
-            )
-            grad = term if grad is None else grad + term
-        grad_hid[pl.ds(start, chunk), :] = grad
+        terms = []
+        for dc in range(3):
+            term = None
+            for dr in range(3):
+                tap = 3 * dr + dc
+                more = dot(
+                    cot_rows[pl.ds(pl.multiple_of(start + (2 - dr) * width, width), chunk), :],
+                    w_conv[:, tap * channels : (tap + 1) * channels],
+                    ((1,), (1,)),
+                )
+                term = more if term is None else term + more
+            terms.append(term)
+        grad_hid[pl.ds(start, chunk), :] = from_neighbours(terms[2], terms[1], terms[0], width)
 
     def backward(r, sums):
         start = pl.multiple_of(r * width, width)
@@ -552,13 +561,15 @@
     def part_of(number):
         return weight_out.at[block_of(number // 4) * 4 + number % 4]
 
-    @pl.loop(0, 16, unroll=True)
-    def _(i):
-        number = lax.rem(high_y * 4 + z_high + i, 16)
-
-        @pl.when(jnp.logical_or(i > 0, jnp.logical_not(gathers)))
-        def _():
-            remote(part_of(number), tile_box.at[rank], send_sem.at[TILE], recv_sem.at[TILE], gatherer(number)).start()
+    for dy, dz in high_steps:
+        number = lax.rem(high_y + dy, 4) * 4 + lax.rem(z_high + dz, 4)
+        copy = remote(
+            part_of(number), tile_box.at[rank], send_sem.at[TILE], recv_sem.at[TILE], gatherer(number)
+        )
+        if dy + dz > 0:
+            copy.start()
+        else:
+            pl.when(jnp.logical_not(gathers))(copy.start)
 
     for m in range(4):
         itself = jnp.logical_and(owns_tail, z_high == m)
@@ -598,27 +609,23 @@
             def _():
                 mod_box[dp] = mod_out[i]
 
-    @pl.loop(0, tile_rows, unroll=True)
-    def _(r):
-        start = pl.multiple_of(r * width, width)
-        column_shifts(hidden[pl.ds(start, width), :].astype(F32), hid_spread, pl.multiple_of(start + width, width), False)
-
-    for tap in range(9):
-        w_stack[tap * channels : (tap + 1) * channels, :] = w_conv[:, tap * channels : (tap + 1) * channels]
-    receive_edges(hidden, hid_edge, 2)
-    column_shifts(hid_edge[0].astype(F32), hid_spread, 0, False)
-    column_shifts(hid_edge[1].astype(F32), hid_spread, pixels + width, False)
+    receive_edges(hid_rows, 2)
 
     @pl.loop(0, 2)
     def _(c):
         start = pl.multiple_of(c * chunk, chunk)
-        conv = merged[pl.ds(start, chunk), :].astype(F32)
-        for dr in range(3):
-            conv = conv + dot(
-                hid_spread[pl.ds(pl.multiple_of(start + dr * width, width), chunk), :],
-                w_stack[3 * dr * channels : 3 * (dr + 1) * channels, :],
-            )
-        out_ref[pl.ds(start, chunk), :] = conv.astype(BF16)
+        terms = []
+        for dc in range(3):
+            term = merged[pl.ds(start, chunk), :].astype(F32) if dc == 1 else None
+            for dr in range(3):
+                tap = 3 * dr + dc
+                more = dot(
+                    hid_rows[pl.ds(pl.multiple_of(start + dr * width, width), chunk), :],
+                    w_conv[:, tap * channels : (tap + 1) * channels],
+                )
+                term = more if term is None else term + more
+            terms.append(term)
+        out_ref[pl.ds(start, chunk), :] = from_neighbours(terms[0], terms[1], terms[2], width).astype(BF16)
 
     stores = [
         pltpu.make_async_copy(source, target, store_sem.at[i])
@@ -637,14 +644,13 @@
     final_slot = 2 * quarter + core
 
     def to_group(rows):
-        @pl.loop(1, n_sp, unroll=True)
-        def _(i):
+        for there in group:
             remote(
                 final_own.at[rows],
                 final_hbm.at[final_slot, rows],
                 send_sem.at[FINAL],
                 recv_sem.at[FINAL],
-                (dp, lax.rem(sp + i, n_sp)),
+                (dp, there),
             ).start()
 
     def own_final(rows):
@@ -697,9 +703,7 @@
         number = from_first // 4
         mod_own[...] = mod_rows[pl.ds(mod_start, share), :].astype(BF16)
 
-        @pl.loop(1, n_sp, unroll=True)
-        def _(i):
-            there = lax.rem(sp + i, n_sp)
+        for there in group:
             remote(mod_own, mod_hbm.at[number], send_sem.at[GRAD_MOD], recv_sem.at[GRAD_MOD], (dp, there)).start()
 
         pltpu.make_async_copy(mod_own, mod_hbm.at[number], store_sem.at[3]).start()
@@ -767,8 +771,8 @@
     def _():
         far.wait_send()
 
-    finish_edges(cot, cot_edge, 0)
-    finish_edges(hidden, hid_edge, 2)
+    finish_edges(cot_rows, 0)
+    finish_edges(hid_rows, 2)
 
     @pl.when(owns_tail)
     def _():
@@ -849,20 +853,15 @@
         vm(w_mod.shape, BF16),
         vm(w_skip.shape, BF16),
         vm(w_conv.shape, BF16),
-        vm((taps * channels, channels), BF16),
-        vm((pixels, channels), BF16),
-        vm((2, width, channels), BF16),
+        vm((pixels + 2 * width, channels), BF16),
         vm((width, half), BF16),
-        vm((2, width, channels), BF16),
         vm((pixels, half), BF16),
         vm((2 * pixels + 2 * width, half), BF16),
-        vm((pixels + 2 * width, 3 * channels), BF16),
         vm((3 * half, 2 * pixels + 2 * width), BF16),
-        vm((pixels + 2 * width, 3 * channels), BF16),
         vm((4 * cells, cells), BF16),
         vm((4 * cells, channels), F32),
         vm((pixels, channels), BF16),
-        vm((pixels, channels), BF16),
+        vm((pixels + 2 * width, channels), BF16),
         vm((2 * pixels, channels), BF16),
         vm((pixels, channels), F32),
         vm((n_sp,) + tile, F32),

time: 55.5 us -> 55.1 us (level)
  no operation moved by 1% of the time
where the time goes in v6:
time: 55.1 us; the launch traced here: 54.9 us
  Pallas kernels  53.6 us (97%)
  between operations  1.29 us (2%)
    pallas_call x1, Pallas kernels, body(): pl.pallas_call(functools.partial(kernel, n_dp, n_sp, tile_rows, width), o...  51.6 us
    pallas_call x1, Pallas kernels, body(): pl.pallas_call(write, out_shape=written, in_specs=[anywhere] * 4, out_spe...  2.08 us

profile of v6, /device:TPU:1, one launch (start us, length us, event | category | flops | bytes accessed | tf_op | source)
XLA Modules:
  0.0 54.9 jit_solution(17548962318471944922)
XLA Ops:
  1.3 51.6 %shard_map.120 = (bf16[1024,256]{1,0:T(8,128)(2,1)}, bf16[1024,256]{1,0:T(8,128)(2,1)}, bf16[8,32,128]{2,1,0:T(8,128)(2,1)}, bf16[4,32,128]{2,1,0:T(8,128)(2,1)}) custom-call(s32[1]{0:T(128)S(6)} %copy.13.refs_0_, s32[32,128]{1,0:T(8,128)} %refs_1_.1, bf16[1024,256]{1,0:T(8,128)(2,1)} %bitcast.5, bf16[64,512]{1,0:T(8,128)(2,1)} %bitcast.7, ...), custom_call_target="tpu_custom_call" | custom-call | tf_op jit(solution)/shard_map/pallas_call | solution.py:906
  52.9 2.1 %shard_map.121 = (bf16[1024,256]{1,0:T(8,128)(2,1)}, bf16[1024,256]{1,0:T(8,128)(2,1)}, bf16[8,2304]{1,0:T(8,128)(2,1)}, bf16[32,512]{1,0:T(8,128)(2,1)}) custom-call(bf16[1024,256]{1,0:T(8,128)(2,1)} %get-tuple-element.12.out, bf16[1024,256]{1,0:T(8,128)(2,1)} %get-tuple-element.13.grad_feat, bf16[8,32,128]{2,1,0:T(8,128)(2,1)} %get-tuple-element.14.final, ...), custom_call_target="tpu_custom_call" | custom-call | tf_op jit(solution)/shard_map/pallas_call | solution.py:926

commit v7 on v6

--- a/solution.py
+++ b/solution.py
@@ -156,7 +156,7 @@
         load(w_mod_hbm, w_mod, 6),
         load(w_conv_hbm, w_conv, 7),
     ]
-    for copy in loads[:2]:
+    for copy in (loads[2], loads[0], loads[1]):
         copy.start()
 
     barrier = pltpu.get_barrier_semaphore()
@@ -172,7 +172,7 @@
     for there in group:
         greet((dp, there))
 
-    for copy in loads[2:] + later:
+    for copy in loads[3:] + later:
         copy.start()
 
     def remote(source, target, send, recv, place):
@@ -216,6 +216,18 @@
 
     def total(box):
         return jnp.sum(box[...], axis=0)
+
+    loads[2].wait()
+    coarse_f = coarse[...].astype(F32)
+    coarse_box[sp] = jnp.concatenate(
+        as_rows(jnp.sum(coarse_f, axis=0, keepdims=True))
+        + as_rows(jnp.sum(coarse_f * coarse_f, axis=0, keepdims=True)),
+        axis=0,
+    )
+
+    pl.semaphore_wait(barrier, jnp.where(owner, n_sp, n_sp + 1))
+
+    to_spatial(coarse_box, COARSE)
 
     vocab = table.shape[0]
     batch, tokens = ids_ref.shape
@@ -239,17 +251,6 @@
             text_rows[:, 8 * j + i, :] = partial[j * n_sp : (j + 1) * n_sp, i * LANES : (i + 1) * LANES]
     text_out[...] = text_rows[...].astype(BF16)
 
-    loads[2].wait()
-    coarse_f = coarse[...].astype(F32)
-    coarse_box[sp] = jnp.concatenate(
-        as_rows(jnp.sum(coarse_f, axis=0, keepdims=True))
-        + as_rows(jnp.sum(coarse_f * coarse_f, axis=0, keepdims=True)),
-        axis=0,
-    )
-
-    pl.semaphore_wait(barrier, jnp.where(owner, n_sp, n_sp + 1))
-
-    to_spatial(coarse_box, COARSE)
     for there in group:
         remote(text_out.at[there], text_box.at[sp], send_sem.at[TEXT], recv_sem.at[TEXT], (dp, there)).start()
 

time: 55.1 us -> 55.3 us (level)
  no operation moved by 1% of the time
where the time goes in v7:
time: 55.3 us; the launch traced here: 55.2 us
  Pallas kernels  53.9 us (97%)
  between operations  1.29 us (2%)
    pallas_call x1, Pallas kernels, body(): pl.pallas_call(functools.partial(kernel, n_dp, n_sp, tile_rows, width), o...  51.8 us
    pallas_call x1, Pallas kernels, body(): pl.pallas_call(write, out_shape=written, in_specs=[anywhere] * 4, out_spe...  2.08 us

profile of v7, /device:TPU:1, one launch (start us, length us, event | category | flops | bytes accessed | tf_op | source)
XLA Modules:
  0.0 55.2 jit_solution(9579891872347942586)
XLA Ops:
  1.3 51.8 %shard_map.120 = (bf16[1024,256]{1,0:T(8,128)(2,1)}, bf16[1024,256]{1,0:T(8,128)(2,1)}, bf16[8,32,128]{2,1,0:T(8,128)(2,1)}, bf16[4,32,128]{2,1,0:T(8,128)(2,1)}) custom-call(s32[1]{0:T(128)S(6)} %copy.13.refs_0_, s32[32,128]{1,0:T(8,128)} %refs_1_.1, bf16[1024,256]{1,0:T(8,128)(2,1)} %bitcast.5, bf16[64,512]{1,0:T(8,128)(2,1)} %bitcast.7, ...), custom_call_target="tpu_custom_call" | custom-call | tf_op jit(solution)/shard_map/pallas_call | solution.py:907
  53.1 2.1 %shard_map.121 = (bf16[1024,256]{1,0:T(8,128)(2,1)}, bf16[1024,256]{1,0:T(8,128)(2,1)}, bf16[8,2304]{1,0:T(8,128)(2,1)}, bf16[32,512]{1,0:T(8,128)(2,1)}) custom-call(bf16[1024,256]{1,0:T(8,128)(2,1)} %get-tuple-element.12.out, bf16[1024,256]{1,0:T(8,128)(2,1)} %get-tuple-element.13.grad_feat, bf16[8,32,128]{2,1,0:T(8,128)(2,1)} %get-tuple-element.14.final, ...), custom_call_target="tpu_custom_call" | custom-call | tf_op jit(solution)/shard_map/pallas_call | solution.py:927
